TPU v7x, 256 devices: a whole 4x4x8 slice. The times are simulated.
256 devices in a mesh: dp: 4 (over x_hi, core), section: 8 (over x_lo, y), tensor: 8 (over z).
Axes of the slice: x: 4 (x_hi: 2, x_lo: 2; x = x_hi * 2 + x_lo), y: 4, z: 8, core: 2. Of those that a mesh axis runs over, the one named last changes fastest.
Arguments:
- text: bfloat16 [8, 64, 8192], P('dp', None, 'tensor'), may hold values from -6 to 6
- order: int32 [4, 2], P('dp'), may hold values from 0 to 1, each once within a row
- lengths: int32 [4, 2], P('dp'), may hold values from 16 to 64
- image: bfloat16 [8, 32, 8192], P('dp', 'section', 'tensor'), may hold values from -6 to 6
- in_gain: float32 [8, 8192], P('section'), may hold values from 0.25 to 1.75
- wq: bfloat16 [8, 8192, 4096], P('section', 'dp', 'tensor'), may hold values from -0.0625 to 0.0625
- wk: bfloat16 [8, 8192, 1024], P('section', 'dp', 'tensor'), may hold values from -0.0625 to 0.0625
- wv: bfloat16 [8, 8192, 1024], P('section', 'dp', 'tensor'), may hold values from -0.0625 to 0.0625
- wo: bfloat16 [8, 4096, 8192], P('section', 'tensor', 'dp'), may hold values from -0.09375 to 0.09375
- query_norm_gain: float32 [8, 128], P('section'), may hold values from 0.5 to 2
- k_gain: float32 [8, 128], P('section'), may hold values from 0.5 to 2
- gate: float32 [8], P('section'), may hold values from -1.5 to 1.5
- cot: bfloat16 [8, 8, 64, 8192], P('section', 'dp'), may hold values from -6 to 6
Outputs:
- states: bfloat16 [8, 8, 64, 8192], P('section', 'dp', None, 'tensor')
- image_grad: float32 [8, 32, 8192], P('dp', 'section', 'tensor')
Inputs may be any that keep to these rules, and one draw needn't show every extreme that they name: `order`: each row lists the 2 micro-batches of one data-parallel group, each once.
All inputs are finite; a program needn't handle non-finite values.
Results may differ from a plain program's by a relative error of at most 0.035.
Values may be sent and summed in bfloat16 or wider, within the bound.
No kernel may reach another device: no remote copies, remote signals or barrier semaphores. Data moves between devices by JAX's collectives and lax.ppermute only.
A program may use at most 128 MiB of HBM per device.

v0:
```python
import functools
import math

import jax
import jax.numpy as jnp
from jax import lax
from jax.experimental import pallas as pl
from jax.experimental.pallas import tpu as pltpu
from jax.sharding import PartitionSpec as P

EPS = 1e-05
HIGH = lax.Precision.HIGHEST
LANES = 128
EXTRA = 16
VMEM_BYTES = 56 * 2**20
ROWS_ROWS = (((1,), (1,)), ((), ()))
COLS_COLS = (((0,), (0,)), ((), ()))


def dot32(a, b, dims=(((1,), (0,)), ((), ()))):
    return lax.dot_general(a, b, dims, precision=HIGH, preferred_element_type=jnp.float32)


def dot16(a, b, dims=(((1,), (0,)), ((), ()))):
    return lax.dot_general(a, b, dims, preferred_element_type=jnp.float32)


def front_kernel(first, last, ints, *refs):
    refs = list(refs)
    text_ref, gain_ref = refs.pop(0), refs.pop(0)
    if not first:
        p_ref, vo_ref, h_ref = refs.pop(0), refs.pop(0), refs.pop(0)
    if not last:
        w_refs = [refs.pop(0) for _ in range(4)]
        q_ref, hq_ref = refs.pop(0), refs.pop(0)
    if not first:
        new_ref = refs.pop(0)
    if not last:
        x_s, ss_s = refs

    def head():
        if first:
            h = text_ref[0]
        else:
            probs = jnp.concatenate([p_ref[i] for i in range(p_ref.shape[0])], axis=1)
            out = dot16(probs, vo_ref[0])
            new = (h_ref[...].astype(jnp.float32) + out).astype(jnp.bfloat16)
            new_ref[...] = new
            if last:
                return
            h = jnp.where(ints[3] > 0, text_ref[0], new)
        hq_ref[...] = h
        hf = h.astype(jnp.float32)
        x_s[...] = (hf * gain_ref[...]).astype(jnp.bfloat16)
        ss = jnp.sum(hf * hf, axis=1, keepdims=True)
        hi = ss.astype(jnp.bfloat16).astype(jnp.float32)
        own, lane = own_lanes(h.shape[0])
        pair = jnp.where(lane < h.shape[0], hi, ss - hi)
        pair = jnp.sum(jnp.where(own, pair, 0.0), axis=0, keepdims=True)
        ss_s[...] = jnp.broadcast_to(pair, ss_s.shape).astype(jnp.bfloat16)

    if last:
        head()
        return
    pl.when(pl.program_id(0) == 0)(head)
    chunk = w_refs[0].shape[1]
    acc = dot16(x_s[:, :chunk], w_refs[0][0])
    for j in range(1, 4):
        acc += dot16(x_s[:, j * chunk : (j + 1) * chunk], w_refs[j][0])
    acc = acc.astype(jnp.bfloat16)
    rows = acc.shape[0]
    for i in range(acc.shape[1] // LANES):
        q_ref[0, i * rows : (i + 1) * rows, :] = acc[:, i * LANES : (i + 1) * LANES]
    q_ref[0, -EXTRA:, :] = ss_s[...]


def own_lanes(rows):
    row = lax.broadcasted_iota(jnp.int32, (rows, LANES), 0)
    lane = lax.broadcasted_iota(jnp.int32, (rows, LANES), 1)
    return (lane == row) | (lane == row + rows), lane


def whole(shape):
    return pl.BlockSpec(shape, lambda *_: (0,) * len(shape))


def front(ints, text, gain, probs, vo, h, w, last=False):
    first = probs is None
    rows, feats = text.shape[1:]
    n, chunk, cols = w[0].shape
    in_specs = [pl.BlockSpec((1, rows, feats), lambda k, i: (i[1], 0, 0)), whole((1, feats))]
    args = [text, gain]
    if not first:
        in_specs += [
            whole(probs.shape),
            pl.BlockSpec((1,) + vo.shape[1:], lambda k, i: (i[0], 0, 0)),
            whole(h.shape),
        ]
        args += [probs, vo, h]
    outs, out_specs, scratch = [], [], []
    state = jax.ShapeDtypeStruct((rows, feats), jnp.bfloat16)
    if not last:
        in_specs += [pl.BlockSpec((1, chunk, cols), lambda k, i: (k, 0, 0))] * 4
        args += list(w)
        part = (cols // LANES * rows + EXTRA, LANES)
        outs += [jax.ShapeDtypeStruct((n,) + part, jnp.bfloat16), state]
        out_specs += [pl.BlockSpec((1,) + part, lambda k, i: (k, 0, 0)), whole((rows, feats))]
        scratch = [pltpu.VMEM((rows, feats), jnp.bfloat16), pltpu.VMEM((EXTRA, LANES), jnp.bfloat16)]
    if not first:
        outs.append(state)
        out_specs.append(whole((rows, feats)))
    return pl.pallas_call(
        functools.partial(front_kernel, first, last),
        grid_spec=pltpu.PrefetchScalarGridSpec(
            num_scalar_prefetch=1,
            grid=(1 if last else n,),
            in_specs=in_specs,
            out_specs=out_specs,
            scratch_shapes=scratch,
        ),
        out_shape=outs,
        compiler_params=pltpu.CompilerParams(vmem_limit_bytes=VMEM_BYTES),
    )(ints, *args)


def attend_kernel(width, ints, alpha_ref, gain_ref, k_ref, q_ref, p_ref, qn_ref):
    total = q_ref[0].astype(jnp.float32)
    for i in range(1, q_ref.shape[0]):
        total += q_ref[i].astype(jnp.float32)
    hd = gain_ref.shape[1]
    rows, cols = qn_ref.shape
    own, _ = own_lanes(rows)
    sums = jnp.broadcast_to(total[cols // hd * rows : cols // hd * rows + 1], (rows, LANES))
    ss = jnp.sum(jnp.where(own, sums, 0.0), axis=1, keepdims=True)
    rs = lax.rsqrt(ss / width + EPS)
    keys = k_ref[0]
    row = lax.broadcasted_iota(jnp.int32, (rows, keys.shape[0]), 0)
    scale = jnp.where(row < ints[2], alpha_ref[0], 0.0)
    parts = []
    for h in range(cols // hd):
        q = total[h * rows : (h + 1) * rows] * rs
        r = lax.rsqrt(jnp.mean(q * q, axis=1, keepdims=True) + EPS)
        qn = q * r * gain_ref[...] * (1.0 / math.sqrt(hd))
        qn_ref[:, h * hd : (h + 1) * hd] = qn
        sc = dot32(qn, keys, ROWS_ROWS)
        e = jnp.exp(sc - jnp.max(sc, axis=1, keepdims=True))
        parts.append(scale * e / jnp.sum(e, axis=1, keepdims=True))
    p_ref[...] = jnp.concatenate(parts, axis=1).astype(jnp.bfloat16)


def attend(ints, alpha, width, gain, keys, parts):
    hd = gain.shape[1]
    toks = keys.shape[1]
    heads = 4
    rows = (parts.shape[1] - EXTRA) // heads
    return pl.pallas_call(
        functools.partial(attend_kernel, width),
        grid_spec=pltpu.PrefetchScalarGridSpec(
            num_scalar_prefetch=1,
            grid=(1,),
            in_specs=[
                pl.BlockSpec(memory_space=pltpu.SMEM),
                whole(gain.shape),
                pl.BlockSpec((1,) + keys.shape[1:], lambda k, i: (i[1], 0, 0)),
                whole(parts.shape),
            ],
            out_specs=[whole((rows, heads * toks)), whole((rows, heads * hd))],
        ),
        out_shape=[
            jax.ShapeDtypeStruct((rows, heads * toks), jnp.bfloat16),
            jax.ShapeDtypeStruct((rows, heads * hd), jnp.float32),
        ],
    )(ints, alpha, gain, keys, parts)


def value_out_kernel(slots, v_ref, *refs):
    w_refs, o_ref = refs[:4], refs[4]
    v = v_ref[0]
    hd = v.shape[1]
    toks = v.shape[0] // slots
    chunk = w_refs[0].shape[2]
    for h in range(w_refs[0].shape[1] // hd):
        for j in range(4):
            r = dot16(v, w_refs[j][0, h * hd : (h + 1) * hd, :]).astype(jnp.bfloat16)
            for o in range(slots):
                o_ref[o, h * toks : (h + 1) * toks, j * chunk : (j + 1) * chunk] = r[
                    o * toks : (o + 1) * toks
                ]


def value_out(v, w, slots):
    n, vrows, hd = v.shape
    heads = w[0].shape[1] // hd
    chunk = w[0].shape[2]
    toks = vrows // slots
    return pl.pallas_call(
        functools.partial(value_out_kernel, slots),
        grid=(n,),
        in_specs=[pl.BlockSpec((1, vrows, hd), lambda k: (k, 0, 0))]
        + [pl.BlockSpec((1,) + w[0].shape[1:], lambda k: (k, 0, 0))] * 4,
        out_specs=pl.BlockSpec((slots, heads * toks, 4 * chunk), lambda k: (0, k, 0)),
        out_shape=jax.ShapeDtypeStruct((slots, n * heads * toks, 4 * chunk), jnp.bfloat16),
        compiler_params=pltpu.CompilerParams(vmem_limit_bytes=VMEM_BYTES),
    )(v, *w)


def back_kernel(qn_ref, k_ref, v_ref, raw_ref, da_ref, gain_ref, o_ref):
    keys, vals, raw, gain = k_ref[0], v_ref[0], raw_ref[0], gain_ref[...]
    hd = keys.shape[1]
    d_kn = jnp.zeros(keys.shape, jnp.float32)
    d_v = jnp.zeros(keys.shape, jnp.float32)
    for h in range(qn_ref.shape[2] // hd):
        qn = qn_ref[0, :, h * hd : (h + 1) * hd]
        da = da_ref[0, :, h * hd : (h + 1) * hd]
        sc = dot32(qn, keys, ROWS_ROWS)
        e = jnp.exp(sc - jnp.max(sc, axis=1, keepdims=True))
        p = e / jnp.sum(e, axis=1, keepdims=True)
        dp = dot32(da, vals, ROWS_ROWS)
        ds = p * (dp - jnp.sum(p * dp, axis=1, keepdims=True))
        d_kn += dot32(ds, qn, COLS_COLS)
        d_v += dot32(p, da, COLS_COLS)
    r = lax.rsqrt(jnp.mean(raw * raw, axis=1, keepdims=True) + EPS)
    u = d_kn * gain
    d_k = r * u - raw * (r * r * r * jnp.mean(raw * u, axis=1, keepdims=True))
    o_ref[0, :, :hd] = d_k.astype(jnp.bfloat16)
    o_ref[0, :, hd:] = d_v.astype(jnp.bfloat16)


def back(qn, keys, vals, raw, da, gain):
    slots, toks, hd = keys.shape
    one = lambda a: pl.BlockSpec((1,) + a.shape[1:], lambda o: (o, 0, 0))
    return pl.pallas_call(
        back_kernel,
        grid=(slots,),
        in_specs=[one(qn), one(keys), one(vals), one(raw), one(da), pl.BlockSpec(gain.shape, lambda o: (0, 0))],
        out_specs=pl.BlockSpec((1, toks, 2 * hd), lambda o: (o, 0, 0)),
        out_shape=jax.ShapeDtypeStruct((slots, toks, 2 * hd), jnp.bfloat16),
    )(qn, keys, vals, raw, da, gain)


def pick(a, i, axis=0):
    return lax.dynamic_index_in_dim(a, i, axis, keepdims=False)


def after(x, *others):
    return lax.optimization_barrier((x,) + others)[0]


def swap(x, axis):
    return lax.all_to_all(x, axis, 0, 0, tiled=True)


def share(x, axis):
    return swap(jnp.broadcast_to(x[None], (lax.axis_size(axis),) + x.shape), axis)


def per_device(
    text, order, lengths, image, in_gain, wq, wk, wv, wo, query_norm_gain, k_gain, gate, cot
):
    D, S, T = lax.axis_size("dp"), lax.axis_size("section"), lax.axis_size("tensor")
    R = T // D
    d, s, t = lax.axis_index("dp"), lax.axis_index("section"), lax.axis_index("tensor")
    slots, rows = text.shape[:2]
    width = in_gain.shape[1]
    hd = k_gain.shape[1]
    feats = width // T
    chunk = feats // D
    toks = image.shape[1] * S

    def onward(x):
        return lax.ppermute(x, "section", [(i, (i + 1) % S) for i in range(S)])

    def dp_flip(x, m):
        return lax.ppermute(x, "dp", [(i, i ^ m) for i in range(D)])

    def dp_all(x):
        across = dp_flip(x, 2)
        return [x, dp_flip(x, 1), across, dp_flip(across, 1)]

    def spread(x):
        parts = jnp.stack(jnp.split(x, D, axis=-1))
        got = swap(jnp.concatenate([parts] * R), "tensor")
        got = pick(got.reshape((D, R) + got.shape[1:]), t // D, 1)
        return jnp.concatenate([pick(got, d ^ j) for j in range(D)], axis=-1)

    def unspread(x, back_sections):
        a, c = t // R, t % D
        parts = jnp.stack(jnp.split(x, D, axis=-1))
        got = []
        for k in range(D):
            pairs = [
                (e * T + b * D + (i + k) % D, (e - back_sections) % S * T + i * R + b)
                for e in range(S)
                for i in range(D)
                for b in range(R)
            ]
            got.append(lax.ppermute(pick(parts, ((c - k) % D) ^ d), ("section", "tensor"), pairs))
        got = jnp.stack(got)
        return jnp.concatenate([pick(got, (j - a) % D) for j in range(D)], axis=-1)

    micro = order[0]
    lens = jnp.take(lengths[0], micro)
    alpha = jnp.tanh(gate)

    img = jnp.moveaxis(share(jnp.take(image, micro, axis=0), "section"), 0, 1)
    img = lax.all_gather(img.reshape(slots * toks, feats), "tensor", axis=1, tiled=True)
    wkv = jnp.concatenate([wk[0], wv[0]], axis=1)
    wkv = lax.all_gather(wkv, "dp", axis=0, tiled=True)
    kv = jnp.dot(img, wkv, preferred_element_type=jnp.float32).reshape(slots, toks, 2 * hd)
    k_raw, vals = kv[..., :hd], kv[..., hd:]
    keys = k_raw * lax.rsqrt(jnp.mean(k_raw * k_raw, axis=-1, keepdims=True) + EPS) * k_gain[0]

    wo_next = onward(wo[0])
    wq_own = swap(wq[0].reshape(T, chunk, wq.shape[2]), "tensor")
    wq_f = dp_all(wq_own)
    text_f = after(jnp.take(text, micro, axis=0), wq_own)
    text_f = spread(text_f)
    gain_f = pick(in_gain.reshape(D, T, chunk), t, 1)
    gain_f = jnp.concatenate([pick(gain_f, d ^ j) for j in range(D)])[None]
    wo_own = jnp.moveaxis(wo_next.reshape(wo.shape[1], T, chunk), 1, 0)
    wo_own = swap(after(wo_own, text_f), "tensor")
    wo_f = dp_all(wo_own)

    probs = h = vo = None
    all_qn, all_h = [], []
    for step in range(S + slots):
        slot_in = jnp.clip(step - s, 0, slots - 1)
        slot_out = jnp.clip(jnp.where(s == 0, step - S, step - s), 0, slots - 1)
        ints = jnp.stack([slot_out, slot_in, lens[slot_in], (s == 0).astype(jnp.int32)])
        last = step == S + slots - 1
        got = front(ints, text_f, gain_f, probs, vo, h, wq_f, last)
        if step > 0:
            all_h.append(got[-1])
        if last:
            break
        parts, hq = got[:2]
        h = onward(hq)
        p, qn = attend(ints, alpha, width, query_norm_gain, keys, swap(parts, "tensor"))
        all_qn.append(qn)
        if step == 0:
            vals16 = vals.astype(jnp.bfloat16).reshape(slots * toks, hd)
            both = share(onward(jnp.concatenate([p, vals16])), "tensor")
            probs = both[:, :rows]
            vo = value_out(both[:, rows:], wo_f, slots)
        else:
            probs = share(onward(p), "tensor")
        if step == 1:
            wo_full = lax.all_gather(after(wo[0], p), "dp", axis=1, tiled=True)

    states = lax.dynamic_slice_in_dim(jnp.stack(all_h), (s - 1) % S, slots, 0)
    states = unspread(states, 1)

    qn = lax.dynamic_slice_in_dim(jnp.stack(all_qn), s, slots, 0)
    mask = (jnp.arange(rows)[None, :] < lens[:, None]).astype(jnp.float32)[:, :, None]
    d_attn = dot16(cot[0].reshape(slots * rows, width), wo_full, ROWS_ROWS)
    d_attn = alpha[0] * mask * d_attn.reshape(slots, rows, -1)
    d_kv = back(qn, keys, vals, k_raw, d_attn, k_gain).reshape(slots * toks, 2 * hd)
    grad = dot16(d_kv, wkv, ROWS_ROWS).astype(jnp.bfloat16)
    grad = swap(jnp.moveaxis(grad.reshape(slots * toks, T, feats), 1, 0), "tensor")
    grad = jnp.sum(grad.astype(jnp.float32), axis=0).astype(jnp.bfloat16)
    grad = swap(jnp.moveaxis(grad.reshape(slots, S, toks // S, feats), 1, 0), "section")
    grad = jnp.sum(grad.astype(jnp.float32), axis=0)
    grad = jnp.stack([pick(grad, jnp.argmax(micro == m)) for m in range(slots)])
    return (states[None], grad)


def solution(mesh):
    return jax.shard_map(
        per_device,
        mesh=mesh,
        in_specs=(
            P("dp", None, "tensor"),
            P("dp", None),
            P("dp", None),
            P("dp", "section", "tensor"),
            P("section", None),
            P("section", "dp", "tensor"),
            P("section", "dp", "tensor"),
            P("section", "dp", "tensor"),
            P("section", "tensor", "dp"),
            P("section", None),
            P("section", None),
            P("section"),
            P("section", "dp", None, None),
        ),
        out_specs=(P("section", "dp", None, "tensor"), P("dp", "section", "tensor")),
        check_vma=False,
    )
```

profile of v0, /device:TPU:32, one launch (start us, length us, event | category | flops | bytes accessed | tf_op | source)
XLA Modules:
  0.0 758.5 jit_solution(10166750464694244608)
XLA Ops:
  11.4 11.8 %all_to_all.120 = bf16[8,2,4,1024]{3,2,1,0:T(4,128)(2,1)S(1)} all-to-all(bf16[8,2,4,1024]{3,2,1,0:T(4,128)(2,1)S(1)} %broadcast_in_dim.51), channel_id=1, replica_groups=mesh['dp'=4,'section'=8,'tensor'=8] {'section'}, dimensions={0} | all-to-all | bytes 262144 | tf_op jit(solution)/shard_map/all_to_all | solution.py:250
  23.2 8.6 %all-to-all-start = ((bf16[8,256,512]{2,1,0:T(8,128)(2,1)}), bf16[8,256,512]{2,1,0:T(8,128)(2,1)}, u32[]{:S(2)}, u32[]{:S(2)}) async-start(bf16[8,256,512]{2,1,0:T(8,128)(2,1)} %bitcast.159), calls=%async_computation | async-start | bytes 4194304 | tf_op jit(solution)/shard_map/all_to_all | solution.py:250
  31.7 4.0 copy.22
  37.6 52.4 %all-to-all-done.refs_2_.refs_5_ = bf16[8,256,512]{2,1,0:T(8,128)(2,1)} async-done(((bf16[8,256,512]{2,1,0:T(8,128)(2,1)}), bf16[8,256,512]{2,1,0:T(8,128)(2,1)}, u32[]{:S(2)}, u32[]{:S(2)}) %all-to-all-start) | async-done | bytes 2097184 | tf_op jit(solution)/shard_map/all_to_all | solution.py:250
  95.1 4.9 all-to-all-start.1
  106.1 8.7 %all-to-all-done.1 = bf16[8,2,64,256]{3,2,1,0:T(8,128)(2,1)S(1)} async-done(((bf16[8,2,64,256]{3,2,1,0:T(8,128)(2,1)}), bf16[8,2,64,256]{3,2,1,0:T(8,128)(2,1)S(1)}, u32[]{:S(2)}, u32[]{:S(2)}) %all-to-all-start.1) | async-done | bytes 524320 | tf_op jit(solution)/shard_map/all_to_all | solution.py:250
  115.6 5.8 all-to-all-start.5
  123.7 45.8 %all-to-all-done.5.refs_0_ = bf16[8,512,256]{2,1,0:T(8,128)(2,1)} async-done(((bf16[8,512,256]{2,1,0:T(8,128)(2,1)}), bf16[8,512,256]{2,1,0:T(8,128)(2,1)}, u32[]{:S(2)}, u32[]{:S(2)}) %all-to-all-start.5) | async-done | bytes 2097184 | tf_op jit(solution)/shard_map/all_to_all | solution.py:250
  172.5 13.1 %collective-permute-done.1.refs_4_.refs_7_ = bf16[8,256,512]{2,1,0:T(8,128)(2,1)} collective-permute-done((bf16[8,256,512]{2,1,0:T(8,128)(2,1)}, bf16[8,256,512]{2,1,0:T(8,128)(2,1)}, u32[]{:S(2)}, u32[]{:S(2)}) %collective-permute-start.1) | collective-permute-done | bytes 2097184 | tf_op jit(solution)/shard_map/ppermute | solution.py:274
  189.0 40.4 %collective-permute-done.6.refs_2_ = bf16[8,512,256]{2,1,0:T(8,128)(2,1)} collective-permute-done((bf16[8,512,256]{2,1,0:T(8,128)(2,1)}, bf16[8,512,256]{2,1,0:T(8,128)(2,1)}, u32[]{:S(2)}, u32[]{:S(2)}) %collective-permute-start.6) | collective-permute-done | bytes 2097184 | tf_op jit(solution)/shard_map/ppermute | solution.py:274
  231.2 8.5 %shard_map.140 = (bf16[8,272,128]{2,1,0:T(8,128)(2,1)}, bf16[64,1024]{1,0:T(8,128)(2,1)}) custom-call(s32[4]{0:T(128)} %add_add_fusion.1.ints, bf16[2,64,1024]{2,1,0:T(8,128)(2,1)} %pad_maximum_fusion.1.refs_0_, f32[1,1024]{1,0:T(1,128)} %bitcast.166, bf16[8,256,512]{2,1,0:T(8,128)(2,1)} %all-to-all-done.refs_2_.refs_5_, ...), custom_call_target="tpu_custom_call" | custom-call | tf_op jit(solution)/shard_map/pallas_call | solution.py:112
  239.7 7.5 all-to-all-start.3
  251.9 12.7 %all-to-all-done.3.q_ref = bf16[8,272,128]{2,1,0:T(8,128)(2,1)S(1)} async-done(((bf16[8,272,128]{2,1,0:T(8,128)(2,1)}), bf16[8,272,128]{2,1,0:T(8,128)(2,1)S(1)}, u32[]{:S(2)}, u32[]{:S(2)}) %all-to-all-start.3) | async-done | bytes 557088 | tf_op jit(solution)/shard_map/all_to_all | solution.py:250
  270.6 4.5 collective-permute-done.3
  275.9 4.8 all-to-all-start.4
  282.0 8.5 %all-to-all-done.4 = bf16[8,128,128]{2,1,0:T(8,128)(2,1)S(1)} async-done(((bf16[8,128,128]{2,1,0:T(8,128)(2,1)}), bf16[8,128,128]{2,1,0:T(8,128)(2,1)S(1)}, u32[]{:S(2)}, u32[]{:S(2)}) %all-to-all-start.4) | async-done | bytes 262176 | tf_op jit(solution)/shard_map/all_to_all | solution.py:250
  291.2 8.5 %shard_map.142.refs_3_ = bf16[2,1024,1024]{2,1,0:T(8,128)(2,1)} custom-call(bf16[8,64,128]{2,1,0:T(8,128)(2,1)} %get-tuple-element.188.v_ref, bf16[8,512,256]{2,1,0:T(8,128)(2,1)} %all-to-all-done.5.refs_0_, bf16[8,512,256]{2,1,0:T(8,128)(2,1)} %collective-permute-done.5.refs_1_, bf16[8,512,256]{2,1,0:T(8,128)(2,1)} %collective-permute-done.6.refs_2_, ...), custom_call_target="tpu_custom_call" | custom-call | tf_op jit(solution)/shard_map/pallas_call | solution.py:196
  300.4 9.6 %shard_map.143 = (bf16[8,272,128]{2,1,0:T(8,128)(2,1)}, bf16[64,1024]{1,0:T(8,128)(2,1)}, bf16[64,1024]{1,0:T(8,128)(2,1)}) custom-call(s32[4]{0:T(128)} %add_add_fusion.ints, bf16[2,64,1024]{2,1,0:T(8,128)(2,1)} %pad_maximum_fusion.1.refs_0_, f32[1,1024]{1,0:T(1,128)} %bitcast.167, bf16[8,64,128]{2,1,0:T(8,128)(2,1)} %get-tuple-element.189.refs_2_, ...), custom_call_target="tpu_custom_call" | custom-call | tf_op jit(solution)/shard_map/pallas_call | solution.py:112
  310.1 20.4 %all_to_all.121.q_ref = bf16[8,272,128]{2,1,0:T(8,128)(2,1)} all-to-all(bf16[8,272,128]{2,1,0:T(8,128)(2,1)} %get-tuple-element.57), channel_id=1, replica_groups=mesh['dp'=4,'section'=8,'tensor'=8] {'tensor'}, dimensions={0} | all-to-all | bytes 1114112 | tf_op jit(solution)/shard_map/all_to_all | solution.py:250
  336.2 4.2 collective-permute-done.9
  341.1 4.7 all-to-all-start.7
  346.5 7.0 all-to-all-done.7
  353.5 9.5 %shard_map.160 = (bf16[9,64,1024]{2,1,0:T(8,128)(2,1)}, bf16[8,272,128]{2,1,0:T(8,128)(2,1)}, bf16[64,1024]{1,0:T(8,128)(2,1)S(1)}) fusion(bf16[9,64,1024]{2,1,0:T(8,128)(2,1)} %bitcast_dynamic-update-slice_fusion.17, s32[4]{0:T(128)S(1)} %add_add_fusion.2, bf16[2,64,1024]{2,1,0:T(8,128)(2,1)S(1)} %copy-done.1, f32[1,1024]{1,0:T(1,128)S(1)} %bitcast.168, ...), kind=kCustom, calls=%fused_computation.28 | custom fusion | bytes 13930512 | tf_op jit(solution)/shard_map/pallas_call | solution.py:112
  363.0 4.9 all-to-all-start.8
  369.2 10.1 %all-to-all-done.8 = bf16[8,272,128]{2,1,0:T(8,128)(2,1)S(1)} async-done(((bf16[8,272,128]{2,1,0:T(8,128)(2,1)}), bf16[8,272,128]{2,1,0:T(8,128)(2,1)S(1)}, u32[]{:S(2)}, u32[]{:S(2)}) %all-to-all-start.8) | async-done | bytes 557088 | tf_op jit(solution)/shard_map/all_to_all | solution.py:250
  381.0 6.2 collective-permute-done.11
  387.9 5.5 all-to-all-start.9
  394.0 6.4 collective-permute-done.12
  401.0 9.0 %shard_map.159 = (bf16[9,64,1024]{2,1,0:T(8,128)(2,1)}, bf16[8,272,128]{2,1,0:T(8,128)(2,1)S(1)}, bf16[64,1024]{1,0:T(8,128)(2,1)S(1)}) fusion(bf16[9,64,1024]{2,1,0:T(8,128)(2,1)} %get-tuple-element.116, s32[4]{0:T(128)S(1)} %add_add_fusion.3, bf16[2,64,1024]{2,1,0:T(8,128)(2,1)S(1)} %copy-done.1, f32[1,1024]{1,0:T(1,128)S(1)} %bitcast.169, ...), kind=kCustom, calls=%fused_computation.27 | custom fusion | bytes 13930512 | tf_op jit(solution)/shard_map/pallas_call | solution.py:112
  410.0 18.6 %all_to_all.122 = bf16[8,272,128]{2,1,0:T(8,128)(2,1)S(1)} all-to-all(bf16[8,272,128]{2,1,0:T(8,128)(2,1)S(1)} %get-tuple-element.111), channel_id=1, replica_groups=mesh['dp'=4,'section'=8,'tensor'=8] {'tensor'}, dimensions={0} | all-to-all | bytes 1114112 | tf_op jit(solution)/shard_map/all_to_all | solution.py:250
  430.4 5.9 collective-permute-done.13
  437.0 4.6 all-to-all-start.11
  442.3 6.4 collective-permute-done.14
  449.3 9.0 %shard_map.158 = (bf16[9,64,1024]{2,1,0:T(8,128)(2,1)}, bf16[8,272,128]{2,1,0:T(8,128)(2,1)S(1)}, bf16[64,1024]{1,0:T(8,128)(2,1)S(1)}) fusion(bf16[9,64,1024]{2,1,0:T(8,128)(2,1)} %get-tuple-element.110, s32[4]{0:T(128)S(1)} %add_add_fusion.4, bf16[2,64,1024]{2,1,0:T(8,128)(2,1)S(1)} %copy-done.1, f32[1,1024]{1,0:T(1,128)S(1)} %bitcast.170, ...), kind=kCustom, calls=%fused_computation.26 | custom fusion | bytes 13930512 | tf_op jit(solution)/shard_map/pallas_call | solution.py:112
  458.3 18.6 %all_to_all.123 = bf16[8,272,128]{2,1,0:T(8,128)(2,1)S(1)} all-to-all(bf16[8,272,128]{2,1,0:T(8,128)(2,1)S(1)} %get-tuple-element.127), channel_id=1, replica_groups=mesh['dp'=4,'section'=8,'tensor'=8] {'tensor'}, dimensions={0} | all-to-all | bytes 1114112 | tf_op jit(solution)/shard_map/all_to_all | solution.py:250
  478.6 5.8 collective-permute-done.15
  485.1 4.7 all-to-all-start.13
  490.6 6.3 collective-permute-done.16
  497.5 9.0 %shard_map.157 = (bf16[9,64,1024]{2,1,0:T(8,128)(2,1)}, bf16[8,272,128]{2,1,0:T(8,128)(2,1)S(1)}, bf16[64,1024]{1,0:T(8,128)(2,1)S(1)}) fusion(bf16[9,64,1024]{2,1,0:T(8,128)(2,1)} %get-tuple-element.126, s32[4]{0:T(128)S(1)} %add_add_fusion.5, bf16[2,64,1024]{2,1,0:T(8,128)(2,1)S(1)} %copy-done.1, f32[1,1024]{1,0:T(1,128)S(1)} %bitcast.171, ...), kind=kCustom, calls=%fused_computation.25 | custom fusion | bytes 13930512 | tf_op jit(solution)/shard_map/pallas_call | solution.py:112
  506.5 18.6 %all_to_all.124 = bf16[8,272,128]{2,1,0:T(8,128)(2,1)S(1)} all-to-all(bf16[8,272,128]{2,1,0:T(8,128)(2,1)S(1)} %get-tuple-element.137), channel_id=1, replica_groups=mesh['dp'=4,'section'=8,'tensor'=8] {'tensor'}, dimensions={0} | all-to-all | bytes 1114112 | tf_op jit(solution)/shard_map/all_to_all | solution.py:250
  526.9 5.8 collective-permute-done.17
  533.4 4.7 all-to-all-start.15
  539.1 6.3 collective-permute-done.18
  545.8 9.0 %shard_map.156 = (bf16[9,64,1024]{2,1,0:T(8,128)(2,1)}, bf16[8,272,128]{2,1,0:T(8,128)(2,1)S(1)}, bf16[64,1024]{1,0:T(8,128)(2,1)S(1)}) fusion(bf16[9,64,1024]{2,1,0:T(8,128)(2,1)} %get-tuple-element.136, s32[4]{0:T(128)S(1)} %add_add_fusion.6, bf16[2,64,1024]{2,1,0:T(8,128)(2,1)S(1)} %copy-done.1, f32[1,1024]{1,0:T(1,128)S(1)} %bitcast.172, ...), kind=kCustom, calls=%fused_computation.24 | custom fusion | bytes 13930512 | tf_op jit(solution)/shard_map/pallas_call | solution.py:112
  554.8 20.2 %all_to_all.125 = bf16[8,272,128]{2,1,0:T(8,128)(2,1)S(1)} all-to-all(bf16[8,272,128]{2,1,0:T(8,128)(2,1)S(1)} %get-tuple-element.143), channel_id=1, replica_groups=mesh['dp'=4,'section'=8,'tensor'=8] {'tensor'}, dimensions={0} | all-to-all | bytes 1114112 | tf_op jit(solution)/shard_map/all_to_all | solution.py:250
  576.7 5.8 collective-permute-done.19
  583.2 4.7 all-to-all-start.17
  588.6 6.4 collective-permute-done.20
  598.3 9.0 %shard_map.155 = (bf16[9,64,1024]{2,1,0:T(8,128)(2,1)}, bf16[8,272,128]{2,1,0:T(8,128)(2,1)S(1)}, bf16[64,1024]{1,0:T(8,128)(2,1)S(1)}) fusion(bf16[9,64,1024]{2,1,0:T(8,128)(2,1)} %get-tuple-element.142, s32[4]{0:T(128)S(1)} %add_add_fusion.7, bf16[2,64,1024]{2,1,0:T(8,128)(2,1)S(1)} %copy-done.1, f32[1,1024]{1,0:T(1,128)S(1)} %bitcast.173, ...), kind=kCustom, calls=%fused_computation.23 | custom fusion | bytes 13930512 | tf_op jit(solution)/shard_map/pallas_call | solution.py:112
  607.3 16.0 %all_to_all.126 = bf16[8,272,128]{2,1,0:T(8,128)(2,1)S(1)} all-to-all(bf16[8,272,128]{2,1,0:T(8,128)(2,1)S(1)} %get-tuple-element.149), channel_id=1, replica_groups=mesh['dp'=4,'section'=8,'tensor'=8] {'tensor'}, dimensions={0} | all-to-all | bytes 1114112 | tf_op jit(solution)/shard_map/all_to_all | solution.py:250
  624.9 5.8 collective-permute-done.21
  631.4 4.7 all-to-all-start.19
  636.9 6.4 collective-permute-done.22
  644.9 9.5 %shard_map.154 = (bf16[9,64,1024]{2,1,0:T(8,128)(2,1)}, bf16[8,272,128]{2,1,0:T(8,128)(2,1)}, bf16[64,1024]{1,0:T(8,128)(2,1)}) fusion(bf16[9,64,1024]{2,1,0:T(8,128)(2,1)} %get-tuple-element.148, s32[4]{0:T(128)S(1)} %add_add_fusion.8, bf16[2,64,1024]{2,1,0:T(8,128)(2,1)S(1)} %copy-done.1, f32[1,1024]{1,0:T(1,128)S(1)} %bitcast.174, ...), kind=kCustom, calls=%fused_computation.22 | custom fusion | bytes 13930512 | tf_op jit(solution)/shard_map/pallas_call | solution.py:112
  654.5 5.5 all-to-all-start.20
  660.1 12.1 %all-to-all-done.20 = bf16[8,272,128]{2,1,0:T(8,128)(2,1)S(1)} async-done(((bf16[8,272,128]{2,1,0:T(8,128)(2,1)}), bf16[8,272,128]{2,1,0:T(8,128)(2,1)S(1)}, u32[]{:S(2)}, u32[]{:S(2)}) %all-to-all-start.20) | async-done | bytes 557088 | tf_op jit(solution)/shard_map/all_to_all | solution.py:250
  675.6 4.2 collective-permute-done.23
  680.4 4.7 all-to-all-start.21
  685.1 4.6 fusion.54
  690.6 5.5 shard_map.145
  700.7 7.2 all-to-all-start.22
  709.3 6.7 collective-permute-done.24
  737.4 7.1 all-to-all-start.23
  746.0 5.0 all-to-all-done.23
  (180 shorter events, 106.8 us)
Async XLA Ops:
  7.2 678.0 %copy-start = (bf16[1,2,64,8192]{3,2,1,0:T(8,128)(2,1)S(1)}, bf16[1,2,64,8192]{3,2,1,0:T(8,128)(2,1)}, u32[]{:S(2)}) copy-start(bf16[1,2,64,8192]{3,2,1,0:T(8,128)(2,1)} %param.25) | copy-start | bytes 6291460
  23.2 66.8 %all-to-all-start = ((bf16[8,256,512]{2,1,0:T(8,128)(2,1)}), bf16[8,256,512]{2,1,0:T(8,128)(2,1)}, u32[]{:S(2)}, u32[]{:S(2)}) async-start(bf16[8,256,512]{2,1,0:T(8,128)(2,1)} %bitcast.159), calls=%async_computation | async-start | bytes 4194304 | tf_op jit(solution)/shard_map/all_to_all | solution.py:250
  31.7 4.5 copy-start.6
  31.7 215.5 %all-gather.4.cloned.1.call-start = ((), (), s32[]{:S(2)}) async-start(), calls=%async_computation.24 | async-start | bytes 1179648 | tf_op jit(solution)/shard_map/all_gather | solution.py:306
  35.7 64.3 %copy-start.4 = (bf16[1,2048,128]{2,1,0:T(8,128)(2,1)S(1)}, bf16[1,2048,128]{2,1,0:T(8,128)(2,1)}, u32[]{:S(2)}) copy-start(bf16[1,2048,128]{2,1,0:T(8,128)(2,1)} %param.20) | copy-start | bytes 1572868
  35.7 66.5 %collective-permute-start.4 = (bf16[512,2048]{0,1:T(8,128)(2,1)}, bf16[512,2048]{0,1:T(8,128)(2,1)}, u32[]{:S(2)}, u32[]{:S(2)}) collective-permute-start(bf16[512,2048]{0,1:T(8,128)(2,1)} %bitcast.155), channel_id=1, source_target_pairs={{0,8},{8,16},{16,24},{24,32},{32,40},{40,48},{48,56},{56,0},{1,9},... | collective-permute-start | bytes 6291464 | tf_op jit(solution)/shard_map/ppermute | solution.py:271
  95.1 19.8 %all-to-all-start.1 = ((bf16[8,2,64,256]{3,2,1,0:T(8,128)(2,1)}), bf16[8,2,64,256]{3,2,1,0:T(8,128)(2,1)S(1)}, u32[]{:S(2)}, u32[]{:S(2)}) async-start(bf16[8,2,64,256]{3,2,1,0:T(8,128)(2,1)} %bitcast_dynamic-update-slice_fusion.19), calls=%async_computation.1 | async-start | bytes 1048576 | tf_op jit(solution)/shard_map/all_to_all | solution.py:250
  99.9 147.3 %all-gather.6.cloned.1.call-start = ((), (), s32[]{:S(2)}) async-start(), calls=%async_computation.25 | async-start | bytes 5242880 | tf_op jit(solution)/shard_map/all_gather | solution.py:308
  115.6 70.6 %copy-start.12 = (f32[1,8192]{1,0:T(1,128)S(1)}, f32[1,8192]{1,0:T(1,128)}, u32[]{:S(2)}) copy-start(f32[1,8192]{1,0:T(1,128)} %param.17) | copy-start | bytes 98308
  115.6 53.8 %all-to-all-start.5 = ((bf16[8,512,256]{2,1,0:T(8,128)(2,1)}), bf16[8,512,256]{2,1,0:T(8,128)(2,1)}, u32[]{:S(2)}, u32[]{:S(2)}) async-start(bf16[8,512,256]{2,1,0:T(8,128)(2,1)} %bitcast.157), calls=%async_computation.5 | async-start | bytes 4194304 | tf_op jit(solution)/shard_map/all_to_all | solution.py:250
  121.4 64.2 %collective-permute-start.1 = (bf16[8,256,512]{2,1,0:T(8,128)(2,1)}, bf16[8,256,512]{2,1,0:T(8,128)(2,1)}, u32[]{:S(2)}, u32[]{:S(2)}) collective-permute-start(bf16[8,256,512]{2,1,0:T(8,128)(2,1)} %all-to-all-done.refs_2_.refs_5_), channel_id=1, source_target_pairs={{0,128},{64,192},{128,0},{192,64},{1,129},{65,193},{129,1},{193,65... | collective-permute-start | bytes 6291464 | tf_op jit(solution)/shard_map/ppermute | solution.py:274
  169.5 59.9 %collective-permute-start.6 = (bf16[8,512,256]{2,1,0:T(8,128)(2,1)}, bf16[8,512,256]{2,1,0:T(8,128)(2,1)}, u32[]{:S(2)}, u32[]{:S(2)}) collective-permute-start(bf16[8,512,256]{2,1,0:T(8,128)(2,1)} %all-to-all-done.5.refs_0_), channel_id=1, source_target_pairs={{0,128},{64,192},{128,0},{192,64},{1,129},{65,193},{129,1},{193,65... | collective-permute-start | bytes 6291464 | tf_op jit(solution)/shard_map/ppermute | solution.py:274
  172.5 58.7 %collective-permute-start = (bf16[8,256,512]{2,1,0:T(8,128)(2,1)}, bf16[8,256,512]{2,1,0:T(8,128)(2,1)}, u32[]{:S(2)}, u32[]{:S(2)}) collective-permute-start(bf16[8,256,512]{2,1,0:T(8,128)(2,1)} %all-to-all-done.refs_2_.refs_5_), channel_id=1, source_target_pairs={{0,64},{64,0},{128,192},{192,128},{1,65},{65,1},{129,193},{193,129... | collective-permute-start | bytes 6291464 | tf_op jit(solution)/shard_map/ppermute | solution.py:274
  185.6 45.6 %collective-permute-start.2 = (bf16[8,256,512]{2,1,0:T(8,128)(2,1)}, bf16[8,256,512]{2,1,0:T(8,128)(2,1)}, u32[]{:S(2)}, u32[]{:S(2)}) collective-permute-start(bf16[8,256,512]{2,1,0:T(8,128)(2,1)} %collective-permute-done.1.refs_4_.refs_7_), channel_id=1, source_target_pairs={{0,64},{64,0},{128,192},{192,128},{1,65},{65,1},{129,193},{193,129... | collective-permute-start | bytes 6291464 | tf_op jit(solution)/shard_map/ppermute | solution.py:274
  188.4 102.8 %collective-permute-start.5 = (bf16[8,512,256]{2,1,0:T(8,128)(2,1)}, bf16[8,512,256]{2,1,0:T(8,128)(2,1)}, u32[]{:S(2)}, u32[]{:S(2)}) collective-permute-start(bf16[8,512,256]{2,1,0:T(8,128)(2,1)} %all-to-all-done.5.refs_0_), channel_id=1, source_target_pairs={{0,64},{64,0},{128,192},{192,128},{1,65},{65,1},{129,193},{193,129... | collective-permute-start | bytes 6291464 | tf_op jit(solution)/shard_map/ppermute | solution.py:274
  229.4 61.8 %collective-permute-start.7 = (bf16[8,512,256]{2,1,0:T(8,128)(2,1)}, bf16[8,512,256]{2,1,0:T(8,128)(2,1)}, u32[]{:S(2)}, u32[]{:S(2)}) collective-permute-start(bf16[8,512,256]{2,1,0:T(8,128)(2,1)} %collective-permute-done.6.refs_2_), channel_id=1, source_target_pairs={{0,64},{64,0},{128,192},{192,128},{1,65},{65,1},{129,193},{193,129... | collective-permute-start | bytes 6291464 | tf_op jit(solution)/shard_map/ppermute | solution.py:274
  239.7 24.9 %all-to-all-start.3 = ((bf16[8,272,128]{2,1,0:T(8,128)(2,1)}), bf16[8,272,128]{2,1,0:T(8,128)(2,1)S(1)}, u32[]{:S(2)}, u32[]{:S(2)}) async-start(bf16[8,272,128]{2,1,0:T(8,128)(2,1)} %get-tuple-element.52), calls=%async_computation.3 | async-start | bytes 1114112 | tf_op jit(solution)/shard_map/all_to_all | solution.py:250
  247.2 4.0 copy-start.13
  247.2 34.8 %copy-start.15 = (bf16[64,1024]{1,0:T(8,128)(2,1)S(1)}, bf16[64,1024]{1,0:T(8,128)(2,1)}, u32[]{:S(2)}) copy-start(bf16[64,1024]{1,0:T(8,128)(2,1)} %get-tuple-element.55) | copy-start | bytes 393220
  269.1 6.0 collective-permute-start.3
  275.9 14.6 %all-to-all-start.4 = ((bf16[8,128,128]{2,1,0:T(8,128)(2,1)}), bf16[8,128,128]{2,1,0:T(8,128)(2,1)S(1)}, u32[]{:S(2)}, u32[]{:S(2)}) async-start(bf16[8,128,128]{2,1,0:T(8,128)(2,1)} %broadcast_in_dim.52), calls=%async_computation.4 | async-start | bytes 524288 | tf_op jit(solution)/shard_map/all_to_all | solution.py:250
  280.7 404.4 %all-gather.8.cloned.1.call-start = ((), (), s32[]{:S(2)}) async-start(), calls=%async_computation.26 | async-start | bytes 10485760 | tf_op jit(solution)/shard_map/all_gather | solution.py:348
  282.0 17.8 %collective-permute-start.8 = (bf16[64,1024]{1,0:T(8,128)(2,1)S(1)}, bf16[64,1024]{1,0:T(8,128)(2,1)S(1)}, u32[]{:S(2)}, u32[]{:S(2)}) collective-permute-start(bf16[64,1024]{1,0:T(8,128)(2,1)S(1)} %copy-done.15), channel_id=1, source_target_pairs={{0,8},{8,16},{16,24},{24,32},{32,40},{40,48},{48,56},{56,0},{1,9},... | collective-permute-start | bytes 393224 | tf_op jit(solution)/shard_map/ppermute | solution.py:271
  310.0 25.3 %copy-start.16 = (bf16[64,1024]{1,0:T(8,128)(2,1)S(1)}, bf16[64,1024]{1,0:T(8,128)(2,1)}, u32[]{:S(2)}) copy-start(bf16[64,1024]{1,0:T(8,128)(2,1)} %get-tuple-element.59) | copy-start | bytes 393220
  310.0 35.8 %copy-start.10 = (bf16[64,1024]{1,0:T(8,128)(2,1)S(1)}, bf16[64,1024]{1,0:T(8,128)(2,1)}, u32[]{:S(2)}) copy-start(bf16[64,1024]{1,0:T(8,128)(2,1)} %get-tuple-element.56) | copy-start | bytes 393220
  310.1 43.4 %copy-start.1 = (bf16[2,64,1024]{2,1,0:T(8,128)(2,1)S(1)}, bf16[2,64,1024]{2,1,0:T(8,128)(2,1)}, u32[]{:S(2)}) copy-start(bf16[2,64,1024]{2,1,0:T(8,128)(2,1)} %pad_maximum_fusion.1.refs_0_) | copy-start | bytes 786436
  310.1 43.4 %copy-start.5 = (f32[1024]{0:T(1024)S(1)}, f32[1024]{0:T(1024)}, u32[]{:S(2)}) copy-start(f32[1024]{0:T(1024)} %pad_maximum_fusion.6) | copy-start | bytes 12292
  334.2 6.2 collective-permute-start.9
  335.3 11.2 %collective-permute-start.10 = (bf16[64,1024]{1,0:T(8,128)(2,1)S(1)}, bf16[64,1024]{1,0:T(8,128)(2,1)S(1)}, u32[]{:S(2)}, u32[]{:S(2)}) collective-permute-start(bf16[64,1024]{1,0:T(8,128)(2,1)S(1)} %copy-done.16), channel_id=1, source_target_pairs={{0,8},{8,16},{16,24},{24,32},{32,40},{40,48},{48,56},{56,0},{1,9},... | collective-permute-start | bytes 393224 | tf_op jit(solution)/shard_map/ppermute | solution.py:271
  341.1 12.4 %all-to-all-start.7 = ((bf16[8,64,128]{2,1,0:T(8,128)(2,1)}), bf16[8,64,128]{2,1,0:T(8,128)(2,1)S(1)}, u32[]{:S(2)}, u32[]{:S(2)}) async-start(bf16[8,64,128]{2,1,0:T(8,128)(2,1)} %broadcast_in_dim.53), calls=%async_computation.7 | async-start | bytes 262144 | tf_op jit(solution)/shard_map/all_to_all | solution.py:250
  346.5 21.4 %copy-start.8 = (f32[64,512]{1,0:T(8,128)S(1)}, f32[64,512]{1,0:T(8,128)}, u32[]{:S(2)}) copy-start(f32[64,512]{1,0:T(8,128)} %get-tuple-element.88) | copy-start | bytes 393220
  346.5 22.1 %copy-start.9 = (f32[64,512]{1,0:T(8,128)S(1)}, f32[64,512]{1,0:T(8,128)}, u32[]{:S(2)}) copy-start(f32[64,512]{1,0:T(8,128)} %get-tuple-element.89) | copy-start | bytes 393220
  346.5 32.8 %copy-start.2 = (f32[2,32,128]{2,1,0:T(8,128)S(1)}, f32[2,32,128]{2,1,0:T(8,128)}, u32[]{:S(2)}) copy-start(f32[2,32,128]{2,1,0:T(8,128)} %multiply_multiply_fusion.k_ref) | copy-start | bytes 98308
  346.5 32.8 %copy-start.11 = (f32[1,128]{1,0:T(1,128)S(1)}, f32[1,128]{1,0:T(1,128)}, u32[]{:S(2)}) copy-start(f32[1,128]{1,0:T(1,128)} %gain_ref.11) | copy-start | bytes 1540
  363.0 16.4 %all-to-all-start.8 = ((bf16[8,272,128]{2,1,0:T(8,128)(2,1)}), bf16[8,272,128]{2,1,0:T(8,128)(2,1)S(1)}, u32[]{:S(2)}, u32[]{:S(2)}) async-start(bf16[8,272,128]{2,1,0:T(8,128)(2,1)} %get-tuple-element.117), calls=%async_computation.8 | async-start | bytes 1114112 | tf_op jit(solution)/shard_map/all_to_all | solution.py:250
  381.0 6.2 collective-permute-start.11
  387.9 13.1 %all-to-all-start.9 = ((bf16[8,64,128]{2,1,0:T(8,128)(2,1)}), bf16[8,64,128]{2,1,0:T(8,128)(2,1)S(1)}, u32[]{:S(2)}, u32[]{:S(2)}) async-start(bf16[8,64,128]{2,1,0:T(8,128)(2,1)} %broadcast_in_dim.54), calls=%async_computation.9 | async-start | bytes 262144 | tf_op jit(solution)/shard_map/all_to_all | solution.py:250
  393.4 7.1 collective-permute-start.12
  430.3 6.0 collective-permute-start.13
  437.0 12.3 %all-to-all-start.11 = ((bf16[8,64,128]{2,1,0:T(8,128)(2,1)}), bf16[8,64,128]{2,1,0:T(8,128)(2,1)S(1)}, u32[]{:S(2)}, u32[]{:S(2)}) async-start(bf16[8,64,128]{2,1,0:T(8,128)(2,1)} %broadcast_in_dim.55), calls=%async_computation.11 | async-start | bytes 262144 | tf_op jit(solution)/shard_map/all_to_all | solution.py:250
  441.6 7.1 collective-permute-start.14
  478.6 5.8 collective-permute-start.15
  485.1 12.4 %all-to-all-start.13 = ((bf16[8,64,128]{2,1,0:T(8,128)(2,1)}), bf16[8,64,128]{2,1,0:T(8,128)(2,1)S(1)}, u32[]{:S(2)}, u32[]{:S(2)}) async-start(bf16[8,64,128]{2,1,0:T(8,128)(2,1)} %broadcast_in_dim.56), calls=%async_computation.13 | async-start | bytes 262144 | tf_op jit(solution)/shard_map/all_to_all | solution.py:250
  489.9 7.1 collective-permute-start.16
  526.9 5.8 collective-permute-start.17
  533.4 12.4 %all-to-all-start.15 = ((bf16[8,64,128]{2,1,0:T(8,128)(2,1)}), bf16[8,64,128]{2,1,0:T(8,128)(2,1)S(1)}, u32[]{:S(2)}, u32[]{:S(2)}) async-start(bf16[8,64,128]{2,1,0:T(8,128)(2,1)} %broadcast_in_dim.57), calls=%async_computation.15 | async-start | bytes 262144 | tf_op jit(solution)/shard_map/all_to_all | solution.py:250
  538.1 7.2 collective-permute-start.18
  576.7 5.8 collective-permute-start.19
  583.2 15.0 %all-to-all-start.17 = ((bf16[8,64,128]{2,1,0:T(8,128)(2,1)}), bf16[8,64,128]{2,1,0:T(8,128)(2,1)S(1)}, u32[]{:S(2)}, u32[]{:S(2)}) async-start(bf16[8,64,128]{2,1,0:T(8,128)(2,1)} %broadcast_in_dim.58), calls=%async_computation.17 | async-start | bytes 262144 | tf_op jit(solution)/shard_map/all_to_all | solution.py:250
  587.9 7.1 collective-permute-start.20
  624.9 5.8 collective-permute-start.21
  631.4 13.5 %all-to-all-start.19 = ((bf16[8,64,128]{2,1,0:T(8,128)(2,1)}), bf16[8,64,128]{2,1,0:T(8,128)(2,1)S(1)}, u32[]{:S(2)}, u32[]{:S(2)}) async-start(bf16[8,64,128]{2,1,0:T(8,128)(2,1)} %broadcast_in_dim.59), calls=%async_computation.19 | async-start | bytes 262144 | tf_op jit(solution)/shard_map/all_to_all | solution.py:250
  636.2 7.1 collective-permute-start.22
  654.5 17.7 %all-to-all-start.20 = ((bf16[8,272,128]{2,1,0:T(8,128)(2,1)}), bf16[8,272,128]{2,1,0:T(8,128)(2,1)S(1)}, u32[]{:S(2)}, u32[]{:S(2)}) async-start(bf16[8,272,128]{2,1,0:T(8,128)(2,1)} %get-tuple-element.159), calls=%async_computation.20 | async-start | bytes 1114112 | tf_op jit(solution)/shard_map/all_to_all | solution.py:250
  673.9 5.8 collective-permute-start.23
  680.4 20.3 %all-to-all-start.21 = ((bf16[8,64,128]{2,1,0:T(8,128)(2,1)}), bf16[8,64,128]{2,1,0:T(8,128)(2,1)S(1)}, u32[]{:S(2)}, u32[]{:S(2)}) async-start(bf16[8,64,128]{2,1,0:T(8,128)(2,1)} %broadcast_in_dim.106), calls=%async_computation.21 | async-start | bytes 262144 | tf_op jit(solution)/shard_map/all_to_all | solution.py:250
  699.7 8.3 %copy-start.14 = (s32[1,2]{1,0:T(1,128)S(1)}, s32[1,2]{1,0:T(1,128)}, u32[]{:S(2)}) copy-start(s32[1,2]{1,0:T(1,128)} %param.14) | copy-start | bytes 28
  700.7 35.7 %all-to-all-start.22 = ((bf16[8,64,1024]{2,1,0:T(8,128)(2,1)}), bf16[8,64,1024]{2,1,0:T(8,128)(2,1)S(1)}, u32[]{:S(2)}, u32[]{:S(2)}) async-start(bf16[8,64,1024]{2,1,0:T(8,128)(2,1)} %bitcast.152), calls=%async_computation.22 | async-start | bytes 2097152 | tf_op jit(solution)/shard_map/all_to_all | solution.py:250
  708.0 8.1 %collective-permute-start.24 = (bf16[64,1024]{1,0:T(8,128)(2,1)}, bf16[64,1024]{1,0:T(8,128)(2,1)}, u32[]{:S(2)}, u32[]{:S(2)}) collective-permute-start(bf16[64,1024]{1,0:T(8,128)(2,1)} %get-tuple-element.161), channel_id=1, source_target_pairs={{0,8},{8,16},{16,24},{24,32},{32,40},{40,48},{48,56},{56,0},{1,9},... | collective-permute-start | bytes 393224 | tf_op jit(solution)/shard_map/ppermute | solution.py:271
  720.4 11.5 %collective-permute-start.28 = (bf16[2,64,256]{2,1,0:T(8,128)(2,1)S(1)}, bf16[2,64,256]{2,1,0:T(8,128)(2,1)S(1)}, u32[]{:S(2)}, u32[]{:S(2)}) collective-permute-start(bf16[2,64,256]{2,1,0:T(8,128)(2,1)S(1)} %get-tuple-element.185), channel_id=1, source_target_pairs={{3,56},{7,57},{0,58},{4,59},{1,60},{5,61},{2,62},{6,63},{11,0},{15... | collective-permute-start | bytes 196616 | tf_op jit(solution)/shard_map/ppermute | solution.py:297
  723.5 9.0 %collective-permute-start.27 = (bf16[2,64,256]{2,1,0:T(8,128)(2,1)S(1)}, bf16[2,64,256]{2,1,0:T(8,128)(2,1)S(1)}, u32[]{:S(2)}, u32[]{:S(2)}) collective-permute-start(bf16[2,64,256]{2,1,0:T(8,128)(2,1)S(1)} %get-tuple-element.186), channel_id=1, source_target_pairs={{2,56},{6,57},{3,58},{7,59},{0,60},{4,61},{1,62},{5,63},{10,0},{14... | collective-permute-start | bytes 196616 | tf_op jit(solution)/shard_map/ppermute | solution.py:297
  723.5 9.9 %collective-permute-start.26 = (bf16[2,64,256]{2,1,0:T(8,128)(2,1)S(1)}, bf16[2,64,256]{2,1,0:T(8,128)(2,1)}, u32[]{:S(2)}, u32[]{:S(2)}) collective-permute-start(bf16[2,64,256]{2,1,0:T(8,128)(2,1)S(1)} %get-tuple-element.187), channel_id=1, source_target_pairs={{1,56},{5,57},{2,58},{6,59},{3,60},{7,61},{0,62},{4,63},{9,0},{13,... | collective-permute-start | bytes 196616 | tf_op jit(solution)/shard_map/ppermute | solution.py:297
  725.4 9.4 %collective-permute-start.25 = (bf16[2,64,256]{2,1,0:T(8,128)(2,1)S(1)}, bf16[2,64,256]{2,1,0:T(8,128)(2,1)}, u32[]{:S(2)}, u32[]{:S(2)}) collective-permute-start(bf16[2,64,256]{2,1,0:T(8,128)(2,1)S(1)} %get-tuple-element.184), channel_id=1, source_target_pairs={{0,56},{4,57},{1,58},{5,59},{2,60},{6,61},{3,62},{7,63},{8,0},{12,... | collective-permute-start | bytes 196616 | tf_op jit(solution)/shard_map/ppermute | solution.py:297
  737.4 13.7 %all-to-all-start.23 = ((bf16[8,2,4,1024]{3,2,1,0:T(4,128)(2,1)}), bf16[8,2,4,1024]{3,2,1,0:T(4,128)(2,1)S(1)}, u32[]{:S(2)}, u32[]{:S(2)}) async-start(bf16[8,2,4,1024]{3,2,1,0:T(4,128)(2,1)} %copy.25), calls=%async_computation.23 | async-start | bytes 262144 | tf_op jit(solution)/shard_map/all_to_all | solution.py:250
  (3 other events, 2.2 us)
Sparse Core Ops, SparseCore 0:
  37.8 48.6 all-gather.3
  102.6 53.7 all-gather.5
  333.7 58.0 all-gather.7
where the time goes:
time: 771 us; the launch traced here: 758 us
  waiting for transfers between devices  319 us (41%)
  blocking collectives  124 us (16%)
  local copies, waits for them, and re-layouts  114 us (15%)
  starting transfers between devices  111 us (14%)
  Pallas kernels  38.1 us (5%)
  other arithmetic  21.8 us (3%)
  between operations  18.9 us (2%)
  matrix products  11.5 us (1%)
    all_to_all x17, waiting for transfers between devices, swap(): return lax.all_to_all(x, axis, 0, 0, tiled=True)  169 us
    all_to_all x7, blocking collectives, swap(): return lax.all_to_all(x, axis, 0, 0, tiled=True)  124 us
    all_to_all x17, starting transfers between devices, swap(): return lax.all_to_all(x, axis, 0, 0, tiled=True)  94.8 us
    ppermute x19, waiting for transfers between devices, onward(): return lax.ppermute(x, 'section', [(i, (i + 1) % S) for i in range(S)])  93.3 us
    pallas_call x8, local copies, waits for them, and re-layouts, front(): pl.pallas_call(functools.partial(front_kernel, first, last), grid_spec=pl...  67.4 us
    ppermute x6, waiting for transfers between devices, dp_flip(): return lax.ppermute(x, 'dp', [(i, i ^ m) for i in range(D)])  53.5 us
    pallas_call x2, Pallas kernels, front(): pl.pallas_call(functools.partial(front_kernel, first, last), grid_spec=pl...  18.1 us
  transfers between devices with their start and end apart: 49, of which 36 were waited for; matrix products, arithmetic and copies ran while one was open for 18% of the time, Pallas kernels for 3%

commit v1 on v0

--- a/solution.py
+++ b/solution.py
@@ -12,7 +12,7 @@
 HIGH = lax.Precision.HIGHEST
 LANES = 128
 EXTRA = 16
-VMEM_BYTES = 56 * 2**20
+VMEM_BYTES = 24 * 2**20
 ROWS_ROWS = (((1,), (1,)), ((), ()))
 COLS_COLS = (((0,), (0,)), ((), ()))
 
@@ -36,42 +36,41 @@
     if not first:
         new_ref = refs.pop(0)
     if not last:
-        x_s, ss_s = refs
-
-    def head():
-        if first:
-            h = text_ref[0]
-        else:
-            probs = jnp.concatenate([p_ref[i] for i in range(p_ref.shape[0])], axis=1)
-            out = dot16(probs, vo_ref[0])
-            new = (h_ref[...].astype(jnp.float32) + out).astype(jnp.bfloat16)
-            new_ref[...] = new
-            if last:
-                return
-            h = jnp.where(ints[3] > 0, text_ref[0], new)
-        hq_ref[...] = h
-        hf = h.astype(jnp.float32)
-        x_s[...] = (hf * gain_ref[...]).astype(jnp.bfloat16)
-        ss = jnp.sum(hf * hf, axis=1, keepdims=True)
-        hi = ss.astype(jnp.bfloat16).astype(jnp.float32)
-        own, lane = own_lanes(h.shape[0])
-        pair = jnp.where(lane < h.shape[0], hi, ss - hi)
-        pair = jnp.sum(jnp.where(own, pair, 0.0), axis=0, keepdims=True)
-        ss_s[...] = jnp.broadcast_to(pair, ss_s.shape).astype(jnp.bfloat16)
-
-    if last:
-        head()
-        return
-    pl.when(pl.program_id(0) == 0)(head)
-    chunk = w_refs[0].shape[1]
-    acc = dot16(x_s[:, :chunk], w_refs[0][0])
-    for j in range(1, 4):
-        acc += dot16(x_s[:, j * chunk : (j + 1) * chunk], w_refs[j][0])
-    acc = acc.astype(jnp.bfloat16)
-    rows = acc.shape[0]
-    for i in range(acc.shape[1] // LANES):
-        q_ref[0, i * rows : (i + 1) * rows, :] = acc[:, i * LANES : (i + 1) * LANES]
-    q_ref[0, -EXTRA:, :] = ss_s[...]
+        x_s = refs.pop(0)
+
+    if first:
+        h = text_ref[ints[1]]
+    else:
+        probs = jnp.concatenate([p_ref[i] for i in range(p_ref.shape[0])], axis=1)
+        new = h_ref[...].astype(jnp.float32) + dot16(probs, vo_ref[ints[0]])
+        new = new.astype(jnp.bfloat16)
+        new_ref[...] = new
+        if last:
+            return
+        h = jnp.where(ints[3] > 0, text_ref[ints[1]], new)
+    hq_ref[...] = h
+    hf = h.astype(jnp.float32)
+    x_s[...] = (hf * gain_ref[...]).astype(jnp.bfloat16)
+    ss = jnp.sum(hf * hf, axis=1, keepdims=True)
+    hi = ss.astype(jnp.bfloat16).astype(jnp.float32)
+    rows = h.shape[0]
+    own, lane = own_lanes(rows)
+    pair = jnp.where(own, jnp.where(lane < rows, hi, ss - hi), 0.0)
+    pair = jnp.broadcast_to(jnp.sum(pair, axis=0, keepdims=True), (EXTRA, LANES))
+    pair = pair.astype(jnp.bfloat16)
+    n, chunk, cols = w_refs[0].shape
+
+    def block(k, carry):
+        acc = dot16(x_s[:, :chunk], w_refs[0][k])
+        for j in range(1, 4):
+            acc += dot16(x_s[:, j * chunk : (j + 1) * chunk], w_refs[j][k])
+        acc = acc.astype(jnp.bfloat16)
+        for i in range(cols // LANES):
+            q_ref[k, i * rows : (i + 1) * rows, :] = acc[:, i * LANES : (i + 1) * LANES]
+        q_ref[k, cols // LANES * rows :, :] = pair
+        return carry
+
+    lax.fori_loop(0, n, block, 0)
 
 
 def own_lanes(rows):
@@ -87,38 +86,26 @@
 def front(ints, text, gain, probs, vo, h, w, last=False):
     first = probs is None
     rows, feats = text.shape[1:]
-    n, chunk, cols = w[0].shape
-    in_specs = [pl.BlockSpec((1, rows, feats), lambda k, i: (i[1], 0, 0)), whole((1, feats))]
+    n, _, cols = w[0].shape
     args = [text, gain]
     if not first:
-        in_specs += [
-            whole(probs.shape),
-            pl.BlockSpec((1,) + vo.shape[1:], lambda k, i: (i[0], 0, 0)),
-            whole(h.shape),
-        ]
         args += [probs, vo, h]
-    outs, out_specs, scratch = [], [], []
+    outs, scratch = [], []
     state = jax.ShapeDtypeStruct((rows, feats), jnp.bfloat16)
     if not last:
-        in_specs += [pl.BlockSpec((1, chunk, cols), lambda k, i: (k, 0, 0))] * 4
         args += list(w)
         part = (cols // LANES * rows + EXTRA, LANES)
         outs += [jax.ShapeDtypeStruct((n,) + part, jnp.bfloat16), state]
-        out_specs += [pl.BlockSpec((1,) + part, lambda k, i: (k, 0, 0)), whole((rows, feats))]
-        scratch = [pltpu.VMEM((rows, feats), jnp.bfloat16), pltpu.VMEM((EXTRA, LANES), jnp.bfloat16)]
+        scratch = [pltpu.VMEM((rows, feats), jnp.bfloat16)]
     if not first:
         outs.append(state)
-        out_specs.append(whole((rows, feats)))
     return pl.pallas_call(
         functools.partial(front_kernel, first, last),
-        grid_spec=pltpu.PrefetchScalarGridSpec(
-            num_scalar_prefetch=1,
-            grid=(1 if last else n,),
-            in_specs=in_specs,
-            out_specs=out_specs,
-            scratch_shapes=scratch,
-        ),
+        in_specs=[pl.BlockSpec(memory_space=pltpu.SMEM)]
+        + [pl.BlockSpec(memory_space=pltpu.VMEM)] * len(args),
+        out_specs=[pl.BlockSpec(memory_space=pltpu.VMEM)] * len(outs),
         out_shape=outs,
+        scratch_shapes=scratch,
         compiler_params=pltpu.CompilerParams(vmem_limit_bytes=VMEM_BYTES),
     )(ints, *args)
 
@@ -175,17 +162,23 @@
 
 def value_out_kernel(slots, v_ref, *refs):
     w_refs, o_ref = refs[:4], refs[4]
-    v = v_ref[0]
-    hd = v.shape[1]
-    toks = v.shape[0] // slots
-    chunk = w_refs[0].shape[2]
-    for h in range(w_refs[0].shape[1] // hd):
-        for j in range(4):
-            r = dot16(v, w_refs[j][0, h * hd : (h + 1) * hd, :]).astype(jnp.bfloat16)
-            for o in range(slots):
-                o_ref[o, h * toks : (h + 1) * toks, j * chunk : (j + 1) * chunk] = r[
-                    o * toks : (o + 1) * toks
-                ]
+    n, vrows, hd = v_ref.shape
+    toks = vrows // slots
+    heads, chunk = w_refs[0].shape[1] // hd, w_refs[0].shape[2]
+
+    def block(k, carry):
+        v = v_ref[k]
+        for h in range(heads):
+            at = pl.multiple_of((k * heads + h) * toks, toks)
+            for j in range(4):
+                r = dot16(v, w_refs[j][k, h * hd : (h + 1) * hd, :]).astype(jnp.bfloat16)
+                for o in range(slots):
+                    o_ref[o, pl.ds(at, toks), j * chunk : (j + 1) * chunk] = r[
+                        o * toks : (o + 1) * toks
+                    ]
+        return carry
+
+    lax.fori_loop(0, n, block, 0)
 
 
 def value_out(v, w, slots):
@@ -195,10 +188,8 @@
     toks = vrows // slots
     return pl.pallas_call(
         functools.partial(value_out_kernel, slots),
-        grid=(n,),
-        in_specs=[pl.BlockSpec((1, vrows, hd), lambda k: (k, 0, 0))]
-        + [pl.BlockSpec((1,) + w[0].shape[1:], lambda k: (k, 0, 0))] * 4,
-        out_specs=pl.BlockSpec((slots, heads * toks, 4 * chunk), lambda k: (0, k, 0)),
+        in_specs=[pl.BlockSpec(memory_space=pltpu.VMEM)] * 5,
+        out_specs=pl.BlockSpec(memory_space=pltpu.VMEM),
         out_shape=jax.ShapeDtypeStruct((slots, n * heads * toks, 4 * chunk), jnp.bfloat16),
         compiler_params=pltpu.CompilerParams(vmem_limit_bytes=VMEM_BYTES),
     )(v, *w)
@@ -302,24 +293,23 @@
     lens = jnp.take(lengths[0], micro)
     alpha = jnp.tanh(gate)
 
-    img = jnp.moveaxis(share(jnp.take(image, micro, axis=0), "section"), 0, 1)
-    img = lax.all_gather(img.reshape(slots * toks, feats), "tensor", axis=1, tiled=True)
     wkv = jnp.concatenate([wk[0], wv[0]], axis=1)
     wkv = lax.all_gather(wkv, "dp", axis=0, tiled=True)
+    img = jnp.moveaxis(share(jnp.take(image, micro, axis=0), "section"), 0, 1)
+    img = after(img.reshape(slots * toks, feats), wkv)
+    img = lax.all_gather(img, "tensor", axis=1, tiled=True)
     kv = jnp.dot(img, wkv, preferred_element_type=jnp.float32).reshape(slots, toks, 2 * hd)
     k_raw, vals = kv[..., :hd], kv[..., hd:]
     keys = k_raw * lax.rsqrt(jnp.mean(k_raw * k_raw, axis=-1, keepdims=True) + EPS) * k_gain[0]
 
     wo_next = onward(wo[0])
-    wq_own = swap(wq[0].reshape(T, chunk, wq.shape[2]), "tensor")
-    wq_f = dp_all(wq_own)
-    text_f = after(jnp.take(text, micro, axis=0), wq_own)
-    text_f = spread(text_f)
+    text_f = spread(jnp.take(text, micro, axis=0))
     gain_f = pick(in_gain.reshape(D, T, chunk), t, 1)
     gain_f = jnp.concatenate([pick(gain_f, d ^ j) for j in range(D)])[None]
+    wq_own = swap(after(wq[0].reshape(T, chunk, wq.shape[2]), text_f), "tensor")
+    wq_f = dp_all(wq_own)
     wo_own = jnp.moveaxis(wo_next.reshape(wo.shape[1], T, chunk), 1, 0)
-    wo_own = swap(after(wo_own, text_f), "tensor")
-    wo_f = dp_all(wo_own)
+    wo_own = swap(after(wo_own, wq_own), "tensor")
 
     probs = h = vo = None
     all_qn, all_h = [], []
@@ -334,6 +324,8 @@
         if last:
             break
         parts, hq = got[:2]
+        if step == 0:
+            wo_f = dp_all(after(wo_own, hq))
         h = onward(hq)
         p, qn = attend(ints, alpha, width, query_norm_gain, keys, swap(parts, "tensor"))
         all_qn.append(qn)
@@ -346,14 +338,16 @@
             probs = share(onward(p), "tensor")
         if step == 1:
             wo_full = lax.all_gather(after(wo[0], p), "dp", axis=1, tiled=True)
+        if step == 5:
+            mask = (jnp.arange(rows)[None, :] < lens[:, None]).astype(jnp.float32)[:, :, None]
+            d_attn = dot16(cot[0].reshape(slots * rows, width), wo_full, ROWS_ROWS)
+            d_attn = alpha[0] * mask * d_attn.reshape(slots, rows, -1)
+            probs, d_attn = lax.optimization_barrier((probs, d_attn))
 
     states = lax.dynamic_slice_in_dim(jnp.stack(all_h), (s - 1) % S, slots, 0)
     states = unspread(states, 1)
 
     qn = lax.dynamic_slice_in_dim(jnp.stack(all_qn), s, slots, 0)
-    mask = (jnp.arange(rows)[None, :] < lens[:, None]).astype(jnp.float32)[:, :, None]
-    d_attn = dot16(cot[0].reshape(slots * rows, width), wo_full, ROWS_ROWS)
-    d_attn = alpha[0] * mask * d_attn.reshape(slots, rows, -1)
     d_kv = back(qn, keys, vals, k_raw, d_attn, k_gain).reshape(slots * toks, 2 * hd)
     grad = dot16(d_kv, wkv, ROWS_ROWS).astype(jnp.bfloat16)
     grad = swap(jnp.moveaxis(grad.reshape(slots * toks, T, feats), 1, 0), "tensor")

time: 771 us -> 761 us (0.987)
  waiting for transfers between devices: 319 us -> 306 us
  blocking collectives: 124 us -> 134 us
  starting transfers between devices: 111 us -> 120 us
    ppermute x6, waiting for transfers between devices: 53.5 us -> 10.9 us  [dp_flip(): return lax.ppermute(x, 'dp', [(i, i ^ m) for i in range(D)])]
    all_gather x1, waiting for transfers between devices: 0.01 us -> 34 us  [per_device(): img = lax.all_gather(img, 'tensor', axis=1, tiled=True)]
    all_to_all x17 -> x18, waiting for transfers between devices: 169 us -> 154 us  [swap(): return lax.all_to_all(x, axis, 0, 0, tiled=True)]
    ppermute x19, waiting for transfers between devices: 93.3 us -> 107 us  [onward(): return lax.ppermute(x, 'section', [(i, (i + 1) % S) for i in range(S)])]
    all_to_all x7 -> x6, blocking collectives: 124 us -> 134 us  [swap(): return lax.all_to_all(x, axis, 0, 0, tiled=True)]
    all_to_all x17 -> x18, starting transfers between devices: 94.8 us -> 98.8 us  [swap(): return lax.all_to_all(x, axis, 0, 0, tiled=True)]
  transfers between devices with their start and end apart: 49 -> 50, of which waited for: 36 -> 34; matrix products, arithmetic and copies ran while one was open for 18% -> 12% of each run, Pallas kernels for 3% -> 3%
where the time goes in v1:
time: 761 us; the launch traced here: 749 us
  waiting for transfers between devices  306 us (40%)
  blocking collectives  134 us (18%)
  starting transfers between devices  120 us (16%)
  local copies, waits for them, and re-layouts  108 us (14%)
  Pallas kernels  32.2 us (4%)
  between operations  19 us (2%)
  other arithmetic  18.3 us (2%)
  matrix products  11.5 us (2%)
    all_to_all x18, waiting for transfers between devices, swap(): return lax.all_to_all(x, axis, 0, 0, tiled=True)  154 us
    all_to_all x6, blocking collectives, swap(): return lax.all_to_all(x, axis, 0, 0, tiled=True)  134 us
    ppermute x19, waiting for transfers between devices, onward(): return lax.ppermute(x, 'section', [(i, (i + 1) % S) for i in range(S)])  107 us
    all_to_all x18, starting transfers between devices, swap(): return lax.all_to_all(x, axis, 0, 0, tiled=True)  98.8 us
    pallas_call x8, local copies, waits for them, and re-layouts, front(): pl.pallas_call(functools.partial(front_kernel, first, last), in_specs=[pl...  61.2 us
    all_gather x1, waiting for transfers between devices, per_device(): img = lax.all_gather(img, 'tensor', axis=1, tiled=True)  34 us
  transfers between devices with their start and end apart: 50, of which 34 were waited for; matrix products, arithmetic and copies ran while one was open for 12% of the time, Pallas kernels for 3%

profile of v1, /device:TPU:32, one launch (start us, length us, event | category | flops | bytes accessed | tf_op | source)
XLA Modules:
  0.0 749.0 jit_solution(2776482541902369471)
XLA Ops:
  16.6 8.6 %all-to-all-start = ((bf16[8,2,64,256]{3,2,1,0:T(8,128)(2,1)}), bf16[8,2,64,256]{3,2,1,0:T(8,128)(2,1)S(1)}, u32[]{:S(2)}, u32[]{:S(2)}) async-start(bf16[8,2,64,256]{3,2,1,0:T(8,128)(2,1)} %constant_dynamic-update-slice_fusion), calls=%async_computation | async-start | bytes 1048576 | tf_op jit(solution)/shard_map/all_to_all | solution.py:241
  25.2 16.0 %all-to-all-done = bf16[8,2,64,256]{3,2,1,0:T(8,128)(2,1)S(1)} async-done(((bf16[8,2,64,256]{3,2,1,0:T(8,128)(2,1)}), bf16[8,2,64,256]{3,2,1,0:T(8,128)(2,1)S(1)}, u32[]{:S(2)}, u32[]{:S(2)}) %all-to-all-start) | async-done | bytes 524320 | tf_op jit(solution)/shard_map/all_to_all | solution.py:241
  41.3 5.8 all-to-all-start.2
  53.8 43.7 %all-to-all-done.2.refs_2_.refs_5_ = bf16[8,256,512]{2,1,0:T(8,128)(2,1)} async-done(((bf16[8,256,512]{2,1,0:T(8,128)(2,1)}), bf16[8,256,512]{2,1,0:T(8,128)(2,1)}, u32[]{:S(2)}, u32[]{:S(2)}) %all-to-all-start.2) | async-done | bytes 2097184 | tf_op jit(solution)/shard_map/all_to_all | solution.py:241
  100.5 25.1 %collective-permute-done.4 = bf16[512,2048]{0,1:T(8,128)(2,1)} collective-permute-done((bf16[512,2048]{0,1:T(8,128)(2,1)}, bf16[512,2048]{0,1:T(8,128)(2,1)}, u32[]{:S(2)}, u32[]{:S(2)}) %collective-permute-start.4) | collective-permute-done | bytes 2097184 | tf_op jit(solution)/shard_map/ppermute | solution.py:262
  129.5 7.4 all-to-all-start.5
  136.9 9.1 %collective-permute-done.1.refs_4_.refs_7_ = bf16[8,256,512]{2,1,0:T(8,128)(2,1)} collective-permute-done((bf16[8,256,512]{2,1,0:T(8,128)(2,1)}, bf16[8,256,512]{2,1,0:T(8,128)(2,1)}, u32[]{:S(2)}, u32[]{:S(2)}) %collective-permute-start.1) | collective-permute-done | bytes 2097184 | tf_op jit(solution)/shard_map/ppermute | solution.py:265
  150.5 6.9 shard_map.140
  157.4 27.3 %all-to-all-done.5.refs_0_ = bf16[8,512,256]{2,1,0:T(8,128)(2,1)} async-done(((bf16[8,512,256]{2,1,0:T(8,128)(2,1)}), bf16[8,512,256]{2,1,0:T(8,128)(2,1)}, u32[]{:S(2)}, u32[]{:S(2)}) %all-to-all-start.5) | async-done | bytes 2097184 | tf_op jit(solution)/shard_map/all_to_all | solution.py:241
  188.2 43.2 %all_to_all.120 = bf16[8,2,4,1024]{3,2,1,0:T(4,128)(2,1)S(1)} all-to-all(bf16[8,2,4,1024]{3,2,1,0:T(4,128)(2,1)S(1)} %broadcast_in_dim.51), channel_id=1, replica_groups=mesh['dp'=4,'section'=8,'tensor'=8] {'section'}, dimensions={0} | all-to-all | bytes 262144 | tf_op jit(solution)/shard_map/all_to_all | solution.py:241
  233.5 7.2 all-to-all-start.3
  240.8 34.0 %all-gather.6.cloned.1.call-done = bf16[64,8192]{1,0:T(8,128)(2,1)} async-done(((bf16[64,1024]{1,0:T(8,128)(2,1)}), bf16[64,8192]{1,0:T(8,128)(2,1)}) %all-gather.6.cloned.1.call-update) | async-done | bytes 1048592 | tf_op jit(solution)/shard_map/all_gather | solution.py:300
  285.1 4.9 collective-permute-done.3
  290.7 4.5 all-to-all-start.4
  296.0 7.9 %all-to-all-done.4 = bf16[8,128,128]{2,1,0:T(8,128)(2,1)S(1)} async-done(((bf16[8,128,128]{2,1,0:T(8,128)(2,1)}), bf16[8,128,128]{2,1,0:T(8,128)(2,1)S(1)}, u32[]{:S(2)}, u32[]{:S(2)}) %all-to-all-start.4) | async-done | bytes 262176 | tf_op jit(solution)/shard_map/all_to_all | solution.py:241
  303.9 5.8 shard_map.142.refs_3_
  309.8 8.0 %shard_map.143 = (bf16[8,272,128]{2,1,0:T(8,128)(2,1)S(1)}, bf16[64,1024]{1,0:T(8,128)(2,1)S(1)}, bf16[64,1024]{1,0:T(8,128)(2,1)S(1)}) custom-call(s32[4]{0:T(128)S(1)} %add_add_fusion.ints, bf16[2,64,1024]{2,1,0:T(8,128)(2,1)S(1)} %pad_maximum_fusion.1.refs_0_, f32[1,1024]{1,0:T(1,128)S(1)} %bitcast.167, ...), custom_call_target="tpu_custom_call" | custom-call | tf_op jit(solution)/shard_map/pallas_call | solution.py:102
  317.8 17.2 %all_to_all.121.q_ref = bf16[8,272,128]{2,1,0:T(8,128)(2,1)} all-to-all(bf16[8,272,128]{2,1,0:T(8,128)(2,1)S(1)} %get-tuple-element.63), channel_id=1, replica_groups=mesh['dp'=4,'section'=8,'tensor'=8] {'tensor'}, dimensions={0} | all-to-all | bytes 1114112 | tf_op jit(solution)/shard_map/all_to_all | solution.py:241
  340.0 4.5 collective-permute-done.9
  345.2 4.8 all-to-all-start.7
  350.7 7.0 all-to-all-done.7
  357.7 8.5 %shard_map.160 = (bf16[9,64,1024]{2,1,0:T(8,128)(2,1)}, bf16[8,272,128]{2,1,0:T(8,128)(2,1)}, bf16[64,1024]{1,0:T(8,128)(2,1)S(1)}) fusion(bf16[9,64,1024]{2,1,0:T(8,128)(2,1)} %bitcast_dynamic-update-slice_fusion.17, s32[4]{0:T(128)S(1)} %add_add_fusion.2, bf16[2,64,1024]{2,1,0:T(8,128)(2,1)S(1)} %pad_maximum_fusion.1.refs_0_, ...), kind=kCustom, calls=%fused_computation.28 | custom fusion | bytes 13930512 | tf_op jit(solution)/shard_map/pallas_call | solution.py:102
  366.2 4.9 all-to-all-start.8
  372.4 10.9 %all-to-all-done.8 = bf16[8,272,128]{2,1,0:T(8,128)(2,1)S(1)} async-done(((bf16[8,272,128]{2,1,0:T(8,128)(2,1)}), bf16[8,272,128]{2,1,0:T(8,128)(2,1)S(1)}, u32[]{:S(2)}, u32[]{:S(2)}) %all-to-all-start.8) | async-done | bytes 557088 | tf_op jit(solution)/shard_map/all_to_all | solution.py:241
  385.0 6.3 collective-permute-done.11
  392.0 4.8 all-to-all-start.9
  397.4 6.4 collective-permute-done.12
  404.4 8.1 %shard_map.159 = (bf16[9,64,1024]{2,1,0:T(8,128)(2,1)}, bf16[8,272,128]{2,1,0:T(8,128)(2,1)S(1)}, bf16[64,1024]{1,0:T(8,128)(2,1)S(1)}) fusion(bf16[9,64,1024]{2,1,0:T(8,128)(2,1)} %get-tuple-element.124, s32[4]{0:T(128)S(1)} %add_add_fusion.3, bf16[2,64,1024]{2,1,0:T(8,128)(2,1)S(1)} %pad_maximum_fusion.1.refs_0_, f32[1,1024]{1,0:T(1,128)S(1)} %bitcast.169, ...), kind=kCustom, calls=%fused_computation.27 | custom fusion | bytes 13930512 | tf_op jit(solution)/shard_map/pallas_call | solution.py:102
  412.5 18.6 %all_to_all.122 = bf16[8,272,128]{2,1,0:T(8,128)(2,1)S(1)} all-to-all(bf16[8,272,128]{2,1,0:T(8,128)(2,1)S(1)} %get-tuple-element.119), channel_id=1, replica_groups=mesh['dp'=4,'section'=8,'tensor'=8] {'tensor'}, dimensions={0} | all-to-all | bytes 1114112 | tf_op jit(solution)/shard_map/all_to_all | solution.py:241
  432.8 6.0 collective-permute-done.13
  439.5 4.6 all-to-all-start.11
  444.8 6.4 collective-permute-done.14
  451.7 8.1 %shard_map.158 = (bf16[9,64,1024]{2,1,0:T(8,128)(2,1)}, bf16[8,272,128]{2,1,0:T(8,128)(2,1)S(1)}, bf16[64,1024]{1,0:T(8,128)(2,1)S(1)}) fusion(bf16[9,64,1024]{2,1,0:T(8,128)(2,1)} %get-tuple-element.118, s32[4]{0:T(128)S(1)} %add_add_fusion.4, bf16[2,64,1024]{2,1,0:T(8,128)(2,1)S(1)} %pad_maximum_fusion.1.refs_0_, f32[1,1024]{1,0:T(1,128)S(1)} %bitcast.170, ...), kind=kCustom, calls=%fused_computation.26 | custom fusion | bytes 13930512 | tf_op jit(solution)/shard_map/pallas_call | solution.py:102
  459.8 18.6 %all_to_all.123 = bf16[8,272,128]{2,1,0:T(8,128)(2,1)S(1)} all-to-all(bf16[8,272,128]{2,1,0:T(8,128)(2,1)S(1)} %get-tuple-element.135), channel_id=1, replica_groups=mesh['dp'=4,'section'=8,'tensor'=8] {'tensor'}, dimensions={0} | all-to-all | bytes 1114112 | tf_op jit(solution)/shard_map/all_to_all | solution.py:241
  480.1 5.8 collective-permute-done.15
  486.6 4.7 all-to-all-start.13
  492.0 6.4 collective-permute-done.16
  499.0 8.5 %shard_map.157 = (bf16[9,64,1024]{2,1,0:T(8,128)(2,1)}, bf16[8,272,128]{2,1,0:T(8,128)(2,1)}, bf16[64,1024]{1,0:T(8,128)(2,1)S(1)}) fusion(bf16[9,64,1024]{2,1,0:T(8,128)(2,1)} %get-tuple-element.134, s32[4]{0:T(128)S(1)} %add_add_fusion.5, bf16[2,64,1024]{2,1,0:T(8,128)(2,1)S(1)} %pad_maximum_fusion.1.refs_0_, f32[1,1024]{1,0:T(1,128)S(1)} %bitcast.171, ...), kind=kCustom, calls=%fused_computation.25 | custom fusion | bytes 13930512 | tf_op jit(solution)/shard_map/pallas_call | solution.py:102
  507.5 6.7 all-to-all-start.14
  514.3 12.1 %all-to-all-done.14 = bf16[8,272,128]{2,1,0:T(8,128)(2,1)S(1)} async-done(((bf16[8,272,128]{2,1,0:T(8,128)(2,1)}), bf16[8,272,128]{2,1,0:T(8,128)(2,1)S(1)}, u32[]{:S(2)}, u32[]{:S(2)}) %all-to-all-start.14) | async-done | bytes 557088 | tf_op jit(solution)/shard_map/all_to_all | solution.py:241
  528.9 5.1 collective-permute-done.17
  534.6 5.1 all-to-all-start.15
  539.8 4.6 fusion.54
  547.7 8.1 %shard_map.156 = (bf16[9,64,1024]{2,1,0:T(8,128)(2,1)}, bf16[8,272,128]{2,1,0:T(8,128)(2,1)S(1)}, bf16[64,1024]{1,0:T(8,128)(2,1)S(1)}) fusion(bf16[9,64,1024]{2,1,0:T(8,128)(2,1)} %get-tuple-element.144, s32[4]{0:T(128)S(1)} %add_add_fusion.6, bf16[2,64,1024]{2,1,0:T(8,128)(2,1)S(1)} %pad_maximum_fusion.1.refs_0_, f32[1,1024]{1,0:T(1,128)S(1)} %bitcast.172, ...), kind=kCustom, calls=%fused_computation.24 | custom fusion | bytes 13930512 | tf_op jit(solution)/shard_map/pallas_call | solution.py:102
  555.8 18.2 %all_to_all.124 = bf16[8,272,128]{2,1,0:T(8,128)(2,1)S(1)} all-to-all(bf16[8,272,128]{2,1,0:T(8,128)(2,1)S(1)} %get-tuple-element.151), channel_id=1, replica_groups=mesh['dp'=4,'section'=8,'tensor'=8] {'tensor'}, dimensions={0} | all-to-all | bytes 1114112 | tf_op jit(solution)/shard_map/all_to_all | solution.py:241
  575.7 5.8 collective-permute-done.19
  582.3 4.7 all-to-all-start.17
  587.7 6.4 collective-permute-done.20
  596.3 8.1 %shard_map.155 = (bf16[9,64,1024]{2,1,0:T(8,128)(2,1)}, bf16[8,272,128]{2,1,0:T(8,128)(2,1)S(1)}, bf16[64,1024]{1,0:T(8,128)(2,1)S(1)}) fusion(bf16[9,64,1024]{2,1,0:T(8,128)(2,1)} %get-tuple-element.150, s32[4]{0:T(128)S(1)} %add_add_fusion.7, bf16[2,64,1024]{2,1,0:T(8,128)(2,1)S(1)} %pad_maximum_fusion.1.refs_0_, f32[1,1024]{1,0:T(1,128)S(1)} %bitcast.173, ...), kind=kCustom, calls=%fused_computation.23 | custom fusion | bytes 13930512 | tf_op jit(solution)/shard_map/pallas_call | solution.py:102
  604.4 18.2 %all_to_all.125 = bf16[8,272,128]{2,1,0:T(8,128)(2,1)S(1)} all-to-all(bf16[8,272,128]{2,1,0:T(8,128)(2,1)S(1)} %get-tuple-element.161), channel_id=1, replica_groups=mesh['dp'=4,'section'=8,'tensor'=8] {'tensor'}, dimensions={0} | all-to-all | bytes 1114112 | tf_op jit(solution)/shard_map/all_to_all | solution.py:241
  624.2 5.8 collective-permute-done.21
  630.7 4.7 all-to-all-start.19
  636.1 6.4 collective-permute-done.22
  643.9 8.5 %shard_map.154 = (bf16[9,64,1024]{2,1,0:T(8,128)(2,1)}, bf16[8,272,128]{2,1,0:T(8,128)(2,1)}, bf16[64,1024]{1,0:T(8,128)(2,1)}) fusion(bf16[9,64,1024]{2,1,0:T(8,128)(2,1)} %get-tuple-element.160, s32[4]{0:T(128)S(1)} %add_add_fusion.8, bf16[2,64,1024]{2,1,0:T(8,128)(2,1)S(1)} %pad_maximum_fusion.1.refs_0_, f32[1,1024]{1,0:T(1,128)S(1)} %bitcast.174, ...), kind=kCustom, calls=%fused_computation.22 | custom fusion | bytes 13930512 | tf_op jit(solution)/shard_map/pallas_call | solution.py:102
  652.4 5.9 all-to-all-start.20
  658.3 12.3 %all-to-all-done.20 = bf16[8,272,128]{2,1,0:T(8,128)(2,1)S(1)} async-done(((bf16[8,272,128]{2,1,0:T(8,128)(2,1)}), bf16[8,272,128]{2,1,0:T(8,128)(2,1)S(1)}, u32[]{:S(2)}, u32[]{:S(2)}) %all-to-all-start.20) | async-done | bytes 557088 | tf_op jit(solution)/shard_map/all_to_all | solution.py:241
  673.9 5.5 shard_map.145
  680.1 4.6 all-to-all-start.21
  689.4 4.0 all-to-all-done.21
  693.4 4.8 all-to-all-start.22
  699.7 5.9 collective-permute-done.24
  715.9 6.1 collective-permute-start.26
  730.0 5.0 all-to-all-start.23
  736.6 5.0 all-to-all-done.23
  (185 shorter events, 105.8 us)
Async XLA Ops:
  7.2 532.6 %copy-start = (bf16[1,2,64,8192]{3,2,1,0:T(8,128)(2,1)S(1)}, bf16[1,2,64,8192]{3,2,1,0:T(8,128)(2,1)}, u32[]{:S(2)}) copy-start(bf16[1,2,64,8192]{3,2,1,0:T(8,128)(2,1)} %param.25) | copy-start | bytes 6291460
  16.6 24.6 %all-to-all-start = ((bf16[8,2,64,256]{3,2,1,0:T(8,128)(2,1)}), bf16[8,2,64,256]{3,2,1,0:T(8,128)(2,1)S(1)}, u32[]{:S(2)}, u32[]{:S(2)}) async-start(bf16[8,2,64,256]{3,2,1,0:T(8,128)(2,1)} %constant_dynamic-update-slice_fusion), calls=%async_computation | async-start | bytes 1048576 | tf_op jit(solution)/shard_map/all_to_all | solution.py:241
  41.3 5.9 copy-start.6
  41.3 5.8 copy-start.7
  41.3 56.2 %all-to-all-start.2 = ((bf16[8,256,512]{2,1,0:T(8,128)(2,1)}), bf16[8,256,512]{2,1,0:T(8,128)(2,1)}, u32[]{:S(2)}, u32[]{:S(2)}) async-start(bf16[8,256,512]{2,1,0:T(8,128)(2,1)} %bitcast.181), calls=%async_computation.2 | async-start | bytes 4194304 | tf_op jit(solution)/shard_map/all_to_all | solution.py:241
  47.1 185.1 %all-gather.4.cloned.1.call-start = ((), (), s32[]{:S(2)}) async-start(), calls=%async_computation.24 | async-start | bytes 5242880 | tf_op jit(solution)/shard_map/all_gather | solution.py:297
  52.2 73.4 %collective-permute-start.4 = (bf16[512,2048]{0,1:T(8,128)(2,1)}, bf16[512,2048]{0,1:T(8,128)(2,1)}, u32[]{:S(2)}, u32[]{:S(2)}) collective-permute-start(bf16[512,2048]{0,1:T(8,128)(2,1)} %bitcast.177), channel_id=1, source_target_pairs={{0,8},{8,16},{16,24},{24,32},{32,40},{40,48},{48,56},{56,0},{1,9},... | collective-permute-start | bytes 6291464 | tf_op jit(solution)/shard_map/ppermute | solution.py:262
  97.5 48.5 %collective-permute-start.1 = (bf16[8,256,512]{2,1,0:T(8,128)(2,1)}, bf16[8,256,512]{2,1,0:T(8,128)(2,1)}, u32[]{:S(2)}, u32[]{:S(2)}) collective-permute-start(bf16[8,256,512]{2,1,0:T(8,128)(2,1)} %all-to-all-done.2.refs_2_.refs_5_), channel_id=1, source_target_pairs={{0,128},{64,192},{128,0},{192,64},{1,129},{65,193},{129,1},{193,65... | collective-permute-start | bytes 6291464 | tf_op jit(solution)/shard_map/ppermute | solution.py:265
  129.5 17.0 %copy-start.15 = (f32[1,8192]{1,0:T(1,128)S(1)}, f32[1,8192]{1,0:T(1,128)}, u32[]{:S(2)}) copy-start(f32[1,8192]{1,0:T(1,128)} %param.17) | copy-start | bytes 98308
  129.5 55.2 %all-to-all-start.5 = ((bf16[8,512,256]{2,1,0:T(8,128)(2,1)}), bf16[8,512,256]{2,1,0:T(8,128)(2,1)}, u32[]{:S(2)}, u32[]{:S(2)}) async-start(bf16[8,512,256]{2,1,0:T(8,128)(2,1)} %bitcast.179), calls=%async_computation.5 | async-start | bytes 4194304 | tf_op jit(solution)/shard_map/all_to_all | solution.py:241
  136.9 137.9 %all-gather.6.cloned.1.call-start = ((), (), s32[]{:S(2)}) async-start(), calls=%async_computation.25 | async-start | bytes 1179648 | tf_op jit(solution)/shard_map/all_gather | solution.py:300
  136.9 11.8 %collective-permute-start = (bf16[8,256,512]{2,1,0:T(8,128)(2,1)}, bf16[8,256,512]{2,1,0:T(8,128)(2,1)}, u32[]{:S(2)}, u32[]{:S(2)}) collective-permute-start(bf16[8,256,512]{2,1,0:T(8,128)(2,1)} %all-to-all-done.2.refs_2_.refs_5_), channel_id=1, source_target_pairs={{0,64},{64,0},{128,192},{192,128},{1,65},{65,1},{129,193},{193,129... | collective-permute-start | bytes 6291464 | tf_op jit(solution)/shard_map/ppermute | solution.py:265
  146.0 4.5 collective-permute-start.2
  148.7 8.7 %copy-start.2 = (s32[4]{0:T(128)}, s32[4]{0:T(128)S(1)}, u32[]{:S(2)}) copy-start(s32[4]{0:T(128)S(1)} %add_add_fusion.1.ints) | copy-start | bytes 52
  150.5 37.0 %copy-start.16 = (bf16[2,4,1024]{2,1,0:T(4,128)(2,1)S(1)}, bf16[2,4,1024]{2,1,0:T(4,128)(2,1)}, u32[]{:S(2)}) copy-start(bf16[2,4,1024]{2,1,0:T(4,128)(2,1)} %param.16) | copy-start | bytes 49156
  184.7 47.6 %collective-permute-start.6 = (bf16[8,512,256]{2,1,0:T(8,128)(2,1)}, bf16[8,512,256]{2,1,0:T(8,128)(2,1)}, u32[]{:S(2)}, u32[]{:S(2)}) collective-permute-start(bf16[8,512,256]{2,1,0:T(8,128)(2,1)} %all-to-all-done.5.refs_0_), channel_id=1, source_target_pairs={{0,128},{64,192},{128,0},{192,64},{1,129},{65,193},{129,1},{193,65... | collective-permute-start | bytes 6291464 | tf_op jit(solution)/shard_map/ppermute | solution.py:265
  232.2 71.6 %collective-permute-start.5 = (bf16[8,512,256]{2,1,0:T(8,128)(2,1)}, bf16[8,512,256]{2,1,0:T(8,128)(2,1)}, u32[]{:S(2)}, u32[]{:S(2)}) collective-permute-start(bf16[8,512,256]{2,1,0:T(8,128)(2,1)} %all-to-all-done.5.refs_0_), channel_id=1, source_target_pairs={{0,64},{64,0},{128,192},{192,128},{1,65},{65,1},{129,193},{193,129... | collective-permute-start | bytes 6291464 | tf_op jit(solution)/shard_map/ppermute | solution.py:265
  232.3 71.5 %collective-permute-start.7 = (bf16[8,512,256]{2,1,0:T(8,128)(2,1)}, bf16[8,512,256]{2,1,0:T(8,128)(2,1)}, u32[]{:S(2)}, u32[]{:S(2)}) collective-permute-start(bf16[8,512,256]{2,1,0:T(8,128)(2,1)} %collective-permute-done.6.refs_2_), channel_id=1, source_target_pairs={{0,64},{64,0},{128,192},{192,128},{1,65},{65,1},{129,193},{193,129... | collective-permute-start | bytes 6291464 | tf_op jit(solution)/shard_map/ppermute | solution.py:265
  233.5 45.9 %all-to-all-start.3 = ((bf16[8,272,128]{2,1,0:T(8,128)(2,1)}), bf16[8,272,128]{2,1,0:T(8,128)(2,1)S(1)}, u32[]{:S(2)}, u32[]{:S(2)}) async-start(bf16[8,272,128]{2,1,0:T(8,128)(2,1)} %get-tuple-element.57), calls=%async_computation.3 | async-start | bytes 1114112 | tf_op jit(solution)/shard_map/all_to_all | solution.py:241
  240.8 38.0 %copy-start.17 = (f32[1,128]{1,0:T(1,128)S(1)}, f32[1,128]{1,0:T(1,128)}, u32[]{:S(2)}) copy-start(f32[1,128]{1,0:T(1,128)} %gain_ref.12) | copy-start | bytes 1540
  284.0 6.0 collective-permute-start.3
  290.7 13.1 %all-to-all-start.4 = ((bf16[8,128,128]{2,1,0:T(8,128)(2,1)}), bf16[8,128,128]{2,1,0:T(8,128)(2,1)S(1)}, u32[]{:S(2)}, u32[]{:S(2)}) async-start(bf16[8,128,128]{2,1,0:T(8,128)(2,1)} %broadcast_in_dim.52), calls=%async_computation.4 | async-start | bytes 524288 | tf_op jit(solution)/shard_map/all_to_all | solution.py:241
  295.2 244.6 %all-gather.8.cloned.1.call-start = ((), (), s32[]{:S(2)}) async-start(), calls=%async_computation.26 | async-start | bytes 10485760 | tf_op jit(solution)/shard_map/all_gather | solution.py:340
  295.9 13.8 %copy-start.3 = (s32[4]{0:T(128)}, s32[4]{0:T(128)S(1)}, u32[]{:S(2)}) copy-start(s32[4]{0:T(128)S(1)} %add_add_fusion.ints) | copy-start | bytes 52
  295.9 13.8 %collective-permute-start.8 = (bf16[64,1024]{1,0:T(8,128)(2,1)S(1)}, bf16[64,1024]{1,0:T(8,128)(2,1)S(1)}, u32[]{:S(2)}, u32[]{:S(2)}) collective-permute-start(bf16[64,1024]{1,0:T(8,128)(2,1)S(1)} %get-tuple-element.60), channel_id=1, source_target_pairs={{0,8},{8,16},{16,24},{24,32},{32,40},{40,48},{48,56},{56,0},{1,9},... | collective-permute-start | bytes 393224 | tf_op jit(solution)/shard_map/ppermute | solution.py:262
  309.7 8.1 %copy-start.1 = (bf16[2,1024,1024]{2,1,0:T(8,128)(2,1)}, bf16[2,1024,1024]{2,1,0:T(8,128)(2,1)S(1)}, u32[]{:S(2)}) copy-start(bf16[2,1024,1024]{2,1,0:T(8,128)(2,1)S(1)} %shard_map.142.refs_3_) | copy-start | bytes 12582916
  338.7 5.8 collective-permute-start.9
  339.4 11.3 %collective-permute-start.10 = (bf16[64,1024]{1,0:T(8,128)(2,1)S(1)}, bf16[64,1024]{1,0:T(8,128)(2,1)S(1)}, u32[]{:S(2)}, u32[]{:S(2)}) collective-permute-start(bf16[64,1024]{1,0:T(8,128)(2,1)S(1)} %get-tuple-element.65), channel_id=1, source_target_pairs={{0,8},{8,16},{16,24},{24,32},{32,40},{40,48},{48,56},{56,0},{1,9},... | collective-permute-start | bytes 393224 | tf_op jit(solution)/shard_map/ppermute | solution.py:262
  345.2 12.5 %all-to-all-start.7 = ((bf16[8,64,128]{2,1,0:T(8,128)(2,1)}), bf16[8,64,128]{2,1,0:T(8,128)(2,1)S(1)}, u32[]{:S(2)}, u32[]{:S(2)}) async-start(bf16[8,64,128]{2,1,0:T(8,128)(2,1)} %broadcast_in_dim.53), calls=%async_computation.7 | async-start | bytes 262144 | tf_op jit(solution)/shard_map/all_to_all | solution.py:241
  350.7 20.4 %copy-start.8 = (f32[64,512]{1,0:T(8,128)S(1)}, f32[64,512]{1,0:T(8,128)}, u32[]{:S(2)}) copy-start(f32[64,512]{1,0:T(8,128)} %get-tuple-element.96) | copy-start | bytes 393220
  350.7 21.1 %copy-start.9 = (f32[64,512]{1,0:T(8,128)S(1)}, f32[64,512]{1,0:T(8,128)}, u32[]{:S(2)}) copy-start(f32[64,512]{1,0:T(8,128)} %get-tuple-element.97) | copy-start | bytes 393220
  350.7 32.6 %copy-start.4 = (f32[2,32,128]{2,1,0:T(8,128)S(1)}, f32[2,32,128]{2,1,0:T(8,128)}, u32[]{:S(2)}) copy-start(f32[2,32,128]{2,1,0:T(8,128)} %multiply_multiply_fusion.k_ref) | copy-start | bytes 98308
  350.7 32.6 %copy-start.14 = (f32[1,128]{1,0:T(1,128)S(1)}, f32[1,128]{1,0:T(1,128)}, u32[]{:S(2)}) copy-start(f32[1,128]{1,0:T(1,128)} %gain_ref.11) | copy-start | bytes 1540
  366.2 17.1 %all-to-all-start.8 = ((bf16[8,272,128]{2,1,0:T(8,128)(2,1)}), bf16[8,272,128]{2,1,0:T(8,128)(2,1)S(1)}, u32[]{:S(2)}, u32[]{:S(2)}) async-start(bf16[8,272,128]{2,1,0:T(8,128)(2,1)} %get-tuple-element.125), calls=%async_computation.8 | async-start | bytes 1114112 | tf_op jit(solution)/shard_map/all_to_all | solution.py:241
  385.0 6.3 collective-permute-start.11
  392.0 12.4 %all-to-all-start.9 = ((bf16[8,64,128]{2,1,0:T(8,128)(2,1)}), bf16[8,64,128]{2,1,0:T(8,128)(2,1)S(1)}, u32[]{:S(2)}, u32[]{:S(2)}) async-start(bf16[8,64,128]{2,1,0:T(8,128)(2,1)} %broadcast_in_dim.54), calls=%async_computation.9 | async-start | bytes 262144 | tf_op jit(solution)/shard_map/all_to_all | solution.py:241
  396.8 7.1 collective-permute-start.12
  432.8 6.0 collective-permute-start.13
  439.5 12.2 %all-to-all-start.11 = ((bf16[8,64,128]{2,1,0:T(8,128)(2,1)}), bf16[8,64,128]{2,1,0:T(8,128)(2,1)S(1)}, u32[]{:S(2)}, u32[]{:S(2)}) async-start(bf16[8,64,128]{2,1,0:T(8,128)(2,1)} %broadcast_in_dim.55), calls=%async_computation.11 | async-start | bytes 262144 | tf_op jit(solution)/shard_map/all_to_all | solution.py:241
  444.1 7.1 collective-permute-start.14
  480.1 5.8 collective-permute-start.15
  486.6 12.4 %all-to-all-start.13 = ((bf16[8,64,128]{2,1,0:T(8,128)(2,1)}), bf16[8,64,128]{2,1,0:T(8,128)(2,1)S(1)}, u32[]{:S(2)}, u32[]{:S(2)}) async-start(bf16[8,64,128]{2,1,0:T(8,128)(2,1)} %broadcast_in_dim.56), calls=%async_computation.13 | async-start | bytes 262144 | tf_op jit(solution)/shard_map/all_to_all | solution.py:241
  491.4 7.1 collective-permute-start.16
  507.5 18.9 %all-to-all-start.14 = ((bf16[8,272,128]{2,1,0:T(8,128)(2,1)}), bf16[8,272,128]{2,1,0:T(8,128)(2,1)S(1)}, u32[]{:S(2)}, u32[]{:S(2)}) async-start(bf16[8,272,128]{2,1,0:T(8,128)(2,1)} %get-tuple-element.145), calls=%async_computation.14 | async-start | bytes 1114112 | tf_op jit(solution)/shard_map/all_to_all | solution.py:241
  528.1 5.8 collective-permute-start.17
  528.8 18.9 %collective-permute-start.18 = (bf16[64,1024]{1,0:T(8,128)(2,1)S(1)}, bf16[64,1024]{1,0:T(8,128)(2,1)S(1)}, u32[]{:S(2)}, u32[]{:S(2)}) collective-permute-start(bf16[64,1024]{1,0:T(8,128)(2,1)S(1)} %get-tuple-element.147), channel_id=1, source_target_pairs={{0,8},{8,16},{16,24},{24,32},{32,40},{40,48},{48,56},{56,0},{1,9},... | collective-permute-start | bytes 393224 | tf_op jit(solution)/shard_map/ppermute | solution.py:262
  534.6 13.0 %all-to-all-start.15 = ((bf16[8,64,128]{2,1,0:T(8,128)(2,1)}), bf16[8,64,128]{2,1,0:T(8,128)(2,1)S(1)}, u32[]{:S(2)}, u32[]{:S(2)}) async-start(bf16[8,64,128]{2,1,0:T(8,128)(2,1)} %broadcast_in_dim.57), calls=%async_computation.15 | async-start | bytes 262144 | tf_op jit(solution)/shard_map/all_to_all | solution.py:241
  575.7 5.8 collective-permute-start.19
  582.3 14.0 %all-to-all-start.17 = ((bf16[8,64,128]{2,1,0:T(8,128)(2,1)}), bf16[8,64,128]{2,1,0:T(8,128)(2,1)S(1)}, u32[]{:S(2)}, u32[]{:S(2)}) async-start(bf16[8,64,128]{2,1,0:T(8,128)(2,1)} %broadcast_in_dim.58), calls=%async_computation.17 | async-start | bytes 262144 | tf_op jit(solution)/shard_map/all_to_all | solution.py:241
  587.0 7.1 collective-permute-start.20
  624.2 5.8 collective-permute-start.21
  630.7 13.2 %all-to-all-start.19 = ((bf16[8,64,128]{2,1,0:T(8,128)(2,1)}), bf16[8,64,128]{2,1,0:T(8,128)(2,1)S(1)}, u32[]{:S(2)}, u32[]{:S(2)}) async-start(bf16[8,64,128]{2,1,0:T(8,128)(2,1)} %broadcast_in_dim.59), calls=%async_computation.19 | async-start | bytes 262144 | tf_op jit(solution)/shard_map/all_to_all | solution.py:241
  635.4 7.1 collective-permute-start.22
  652.4 18.1 %all-to-all-start.20 = ((bf16[8,272,128]{2,1,0:T(8,128)(2,1)}), bf16[8,272,128]{2,1,0:T(8,128)(2,1)S(1)}, u32[]{:S(2)}, u32[]{:S(2)}) async-start(bf16[8,272,128]{2,1,0:T(8,128)(2,1)} %get-tuple-element.171), calls=%async_computation.20 | async-start | bytes 1114112 | tf_op jit(solution)/shard_map/all_to_all | solution.py:241
  672.3 7.2 collective-permute-start.23
  680.1 13.3 %all-to-all-start.21 = ((bf16[8,64,128]{2,1,0:T(8,128)(2,1)}), bf16[8,64,128]{2,1,0:T(8,128)(2,1)S(1)}, u32[]{:S(2)}, u32[]{:S(2)}) async-start(bf16[8,64,128]{2,1,0:T(8,128)(2,1)} %broadcast_in_dim.106), calls=%async_computation.21 | async-start | bytes 262144 | tf_op jit(solution)/shard_map/all_to_all | solution.py:241
  688.3 9.9 %copy-start.18 = (s32[1,2]{1,0:T(1,128)S(1)}, s32[1,2]{1,0:T(1,128)}, u32[]{:S(2)}) copy-start(s32[1,2]{1,0:T(1,128)} %param.14) | copy-start | bytes 28
  693.4 35.7 %all-to-all-start.22 = ((bf16[8,64,1024]{2,1,0:T(8,128)(2,1)}), bf16[8,64,1024]{2,1,0:T(8,128)(2,1)S(1)}, u32[]{:S(2)}, u32[]{:S(2)}) async-start(bf16[8,64,1024]{2,1,0:T(8,128)(2,1)} %bitcast.164), calls=%async_computation.22 | async-start | bytes 2097152 | tf_op jit(solution)/shard_map/all_to_all | solution.py:241
  698.2 7.4 collective-permute-start.24
  710.6 16.1 %collective-permute-start.25 = (bf16[2,64,256]{2,1,0:T(8,128)(2,1)}, bf16[2,64,256]{2,1,0:T(8,128)(2,1)S(1)}, u32[]{:S(2)}, u32[]{:S(2)}) collective-permute-start(bf16[2,64,256]{2,1,0:T(8,128)(2,1)} %get-tuple-element.192), channel_id=1, source_target_pairs={{0,56},{4,57},{1,58},{5,59},{2,60},{6,61},{3,62},{7,63},{8,0},{12,... | collective-permute-start | bytes 196616 | tf_op jit(solution)/shard_map/ppermute | solution.py:288
  713.2 13.5 %collective-permute-start.28 = (bf16[2,64,256]{2,1,0:T(8,128)(2,1)}, bf16[2,64,256]{2,1,0:T(8,128)(2,1)S(1)}, u32[]{:S(2)}, u32[]{:S(2)}) collective-permute-start(bf16[2,64,256]{2,1,0:T(8,128)(2,1)} %get-tuple-element.193), channel_id=1, source_target_pairs={{3,56},{7,57},{0,58},{4,59},{1,60},{5,61},{2,62},{6,63},{11,0},{15... | collective-permute-start | bytes 196616 | tf_op jit(solution)/shard_map/ppermute | solution.py:288
  715.9 10.8 %collective-permute-start.27 = (bf16[2,64,256]{2,1,0:T(8,128)(2,1)S(1)}, bf16[2,64,256]{2,1,0:T(8,128)(2,1)S(1)}, u32[]{:S(2)}, u32[]{:S(2)}) collective-permute-start(bf16[2,64,256]{2,1,0:T(8,128)(2,1)S(1)} %get-tuple-element.194), channel_id=1, source_target_pairs={{2,56},{6,57},{3,58},{7,59},{0,60},{4,61},{1,62},{5,63},{10,0},{14... | collective-permute-start | bytes 196616 | tf_op jit(solution)/shard_map/ppermute | solution.py:288
  715.9 10.8 %collective-permute-start.26 = (bf16[2,64,256]{2,1,0:T(8,128)(2,1)S(1)}, bf16[2,64,256]{2,1,0:T(8,128)(2,1)S(1)}, u32[]{:S(2)}, u32[]{:S(2)}) collective-permute-start(bf16[2,64,256]{2,1,0:T(8,128)(2,1)S(1)} %get-tuple-element.195), channel_id=1, source_target_pairs={{1,56},{5,57},{2,58},{6,59},{3,60},{7,61},{0,62},{4,63},{9,0},{13,... | collective-permute-start | bytes 196616 | tf_op jit(solution)/shard_map/ppermute | solution.py:288
  730.0 11.6 %all-to-all-start.23 = ((bf16[8,2,4,1024]{3,2,1,0:T(4,128)(2,1)}), bf16[8,2,4,1024]{3,2,1,0:T(4,128)(2,1)S(1)}, u32[]{:S(2)}, u32[]{:S(2)}) async-start(bf16[8,2,4,1024]{3,2,1,0:T(4,128)(2,1)} %copy.25), calls=%async_computation.23 | async-start | bytes 262144 | tf_op jit(solution)/shard_map/all_to_all | solution.py:241
  (6 other events, 4.0 us)
Sparse Core Ops, SparseCore 0:
  49.8 42.3 all-gather.3
  232.4 42.3 all-gather.5
  338.1 59.7 all-gather.7
